TPU v7x, 32 devices: a whole 2x2x4 slice. The times are simulated.
32 devices in a mesh: dom: 16 (over z, y, x), feat: 2 (over core).
Axes of the slice: x: 2, y: 2, z: 4, core: 2. Of those that a mesh axis runs over, the one named last changes fastest.
Arguments:
- features: bfloat16 [32768, 100], P('dom', 'feat'), may hold values from -6 to 6
- local_mask: int32 [32768, 2048], P('dom'), may hold values 0 or 1
- halo_mask: int32 [32768, 128], P('dom'), may hold values 0 or 1
- send_rows: int32 [16, 16, 8], P('dom'), may hold values from 0 to 2047
- labels: int32 [32768], P('dom'), may hold values from 0 to 46
- label_mask: int32 [32768], P('dom'), may hold values from 0 to 1
- master: float32 [2, 103680], P('feat', 'dom')
- first_moment: float32 [2, 103680], P('feat', 'dom'), may hold values from -0.00390625 to 0.00390625
- second_moment: float32 [2, 103680], P('feat', 'dom'), may hold values from 6.866455e-09 to 2.746582e-08
Outputs:
- loss_sum: float32 [], replicated
- label_count: float32 [], replicated
- new_master: float32 [2, 103680], P('feat', 'dom')
- new_first: float32 [2, 103680], P('feat', 'dom')
- new_second: float32 [2, 103680], P('feat', 'dom')
All inputs are finite; a program needn't handle non-finite values. No bound on the sum of `local_mask` or of `halo_mask` on one device may be relied on, other than what follows from the above.
Results may differ from a plain program's by a relative error of at most 0.0005.
The roundings to bfloat16 on the way count: a program that leaves them out, or rounds other values in their place, can miss the bound.
Values may be sent and summed in bfloat16 or wider, within the bound.
A program may use at most 128 MiB of HBM per device.

v0:
```python
import jax
import jax.numpy as jnp
from jax import lax
from jax.sharding import PartitionSpec as P

HID = 256
CLS = 47
STEP = 10


EPSILON = 1e-05
LEARN_RATE = 0.02
DECAY_ONE = 0.9
DECAY_TWO = 0.999
ADAM_EPS = 1e-08
WEIGHT_DECAY = 0.01


def product(matrix_a, matrix_b):
    return jnp.dot(matrix_a, matrix_b, preferred_element_type=jnp.float32)


def contract_rows(matrix_a, matrix_b):
    return lax.dot_general(
        matrix_a, matrix_b, (((0,), (0,)), ((), ())), preferred_element_type=jnp.float32
    )


def contract_cols(matrix_a, matrix_b):
    return lax.dot_general(
        matrix_a, matrix_b, (((1,), (1,)), ((), ())), preferred_element_type=jnp.float32
    )


def unpack(flat_params, inner_width, hidden_width):
    edge_one = 2 * inner_width * HID
    edge_two = edge_one + 2 * hidden_width * HID
    edge_three = edge_two + 2 * hidden_width * CLS
    layer_one = flat_params[:edge_one].reshape(2, inner_width, HID)
    layer_two = flat_params[edge_one:edge_two].reshape(2, hidden_width, HID)
    head_part = flat_params[edge_two:edge_three].reshape(2, hidden_width, CLS)
    norm_part = flat_params[edge_three:].reshape(4, hidden_width)
    matrices = [
        (layer_one[0], layer_one[1]),
        (layer_two[0], layer_two[1]),
        (head_part[0], head_part[1]),
    ]
    return (matrices, norm_part)


def layer_forward(states, weight_pair, graph, is_head):
    local_adj, halo_adj, inverse, send_index = graph
    outgoing = jnp.take(states, send_index, axis=0)
    incoming = lax.all_to_all(outgoing, "dom", split_axis=0, concat_axis=0, tiled=True)
    halo_feats = incoming.reshape(-1, states.shape[1])
    summed = product(local_adj, states) + product(halo_adj, halo_feats)
    aggregated = (summed * inverse[:, None]).astype(jnp.bfloat16)
    if is_head:
        partial_value = product(states, weight_pair[0]) + product(aggregated, weight_pair[1])
        mixed = lax.psum(partial_value, "feat")
    else:
        partial_value = product(states, weight_pair[0]) + product(aggregated, weight_pair[1])
        mixed = lax.psum_scatter(partial_value, "feat", scatter_dimension=1, tiled=True)
    return (mixed, aggregated)


def norm_forward(mixed, gain, shift):
    totals = lax.psum((jnp.sum(mixed, axis=1), jnp.sum(mixed * mixed, axis=1)), "feat")
    centre_mean = totals[0] / HID
    variance = totals[1] / HID - centre_mean * centre_mean
    scale_inv = lax.rsqrt(variance + EPSILON)
    normed = (mixed - centre_mean[:, None]) * scale_inv[:, None]
    shifted = normed * gain + shift
    return (jax.nn.gelu(shifted).astype(jnp.bfloat16), (normed, scale_inv, shifted))


def norm_backward(grad_out, kept, gain):
    normed, scale_inv, shifted = kept
    unused, gelu_back = jax.vjp(jax.nn.gelu, shifted)
    grad_shift = gelu_back(grad_out)[0]
    grad_gain = jnp.sum(grad_shift * normed, axis=0)
    grad_bias = jnp.sum(grad_shift, axis=0)
    grad_normed = grad_shift * gain
    totals = lax.psum((jnp.sum(grad_normed, axis=1), jnp.sum(grad_normed * normed, axis=1)), "feat")
    grad_mixed = scale_inv[:, None] * (
        grad_normed - totals[0][:, None] / HID - normed * totals[1][:, None] / HID
    )
    return (grad_mixed, grad_gain, grad_bias)


def layer_backward(grad_full, states, aggregated, weight_pair, graph, needs_input):
    grad_self = contract_rows(states, grad_full)
    grad_neigh = contract_rows(aggregated, grad_full)
    if not needs_input:
        return (grad_self, grad_neigh, None)
    local_adj, halo_adj, inverse, send_index = graph
    grad_states = contract_cols(grad_full, weight_pair[0])
    grad_agg = contract_cols(grad_full, weight_pair[1])
    grad_summed = (grad_agg * inverse[:, None]).astype(jnp.bfloat16)
    grad_states = grad_states + contract_rows(local_adj, grad_summed)
    grad_halo = contract_rows(halo_adj, grad_summed).astype(jnp.bfloat16)
    returned = lax.all_to_all(
        grad_halo.reshape(send_index.shape + (-1,)), "dom", split_axis=0, concat_axis=0, tiled=True
    )
    flat_back = returned.reshape(-1, returned.shape[-1]).astype(jnp.float32)
    grad_states = grad_states.at[send_index.reshape(-1)].add(flat_back)
    return (grad_self, grad_neigh, grad_states)


def per_device(
    features,
    local_mask,
    halo_mask,
    send_rows,
    labels,
    label_mask,
    master,
    first_moment,
    second_moment,
):
    gathered = lax.all_gather(master.astype(jnp.bfloat16), "dom", axis=1, tiled=True)
    inner_width = features.shape[1]
    hidden_width = HID // lax.axis_size("feat")
    matrices, norm_part = unpack(gathered[0], inner_width, hidden_width)
    norm_float = norm_part.astype(jnp.float32)
    local_adj = local_mask.astype(jnp.bfloat16)
    halo_adj = halo_mask.astype(jnp.bfloat16)
    degree = jnp.sum(local_mask, axis=1) + jnp.sum(halo_mask, axis=1)
    inverse = 1.0 / jnp.maximum(degree, 1).astype(jnp.float32)
    graph = (local_adj, halo_adj, inverse, send_rows[0])
    weight_mask = label_mask.astype(jnp.float32)
    states = features
    inputs_kept = []
    norms_kept = []
    for number in range(3):
        mixed, aggregated = layer_forward(states, matrices[number], graph, number == 2)
        inputs_kept.append((states, aggregated))
        if number < 2:
            states, kept = norm_forward(mixed, norm_float[2 * number], norm_float[2 * number + 1])
            norms_kept.append(kept)
    log_total = jax.nn.logsumexp(mixed, axis=1)
    classes = lax.broadcasted_iota(jnp.int32, mixed.shape, 1)
    onehot = (classes == labels[:, None]).astype(jnp.float32)
    picked = jnp.sum(mixed * onehot, axis=1)
    loss_sum, label_count = lax.psum(
        (jnp.sum((log_total - picked) * weight_mask), jnp.sum(weight_mask)), "dom"
    )
    probs = jnp.exp(mixed - log_total[:, None])
    grad_full = ((probs - onehot) * (weight_mask / label_count)[:, None]).astype(jnp.bfloat16)
    weight_grads = [None, None, None]
    norm_grads = [None, None]
    for number in (2, 1, 0):
        states, aggregated = inputs_kept[number]
        grad_self, grad_neigh, grad_states = layer_backward(
            grad_full, states, aggregated, matrices[number], graph, number > 0
        )
        weight_grads[number] = (grad_self, grad_neigh)
        if number > 0:
            grad_mixed, grad_gain, grad_bias = norm_backward(
                grad_states, norms_kept[number - 1], norm_float[2 * number - 2]
            )
            norm_grads[number - 1] = (grad_gain, grad_bias)
            grad_full = lax.all_gather(grad_mixed.astype(jnp.bfloat16), "feat", axis=1, tiled=True)
    pieces = [
        weight_grads[0][0],
        weight_grads[0][1],
        weight_grads[1][0],
        weight_grads[1][1],
        weight_grads[2][0],
        weight_grads[2][1],
        norm_grads[0][0],
        norm_grads[0][1],
        norm_grads[1][0],
        norm_grads[1][1],
    ]
    gradient = jnp.concatenate([piece.reshape(-1) for piece in pieces])[None, :]
    shard_width = master.shape[1]
    summed_all = lax.psum(gradient, "dom")
    own_grad = lax.dynamic_slice_in_dim(
        summed_all, lax.axis_index("dom") * shard_width, shard_width, 1
    )
    new_first = DECAY_ONE * first_moment + (1.0 - DECAY_ONE) * own_grad
    new_second = DECAY_TWO * second_moment + (1.0 - DECAY_TWO) * own_grad * own_grad
    first_hat = new_first / (1.0 - DECAY_ONE**STEP)
    second_hat = new_second / (1.0 - DECAY_TWO**STEP)
    new_master = master - LEARN_RATE * (
        first_hat / (jnp.sqrt(second_hat) + ADAM_EPS) + WEIGHT_DECAY * master
    )
    return (loss_sum, label_count, new_master, new_first, new_second)


def solution(mesh):
    in_specs = (
        P("dom", "feat"),
        P("dom", None),
        P("dom", None),
        P("dom", None, None),
        P("dom"),
        P("dom"),
        P("feat", "dom"),
        P("feat", "dom"),
        P("feat", "dom"),
    )
    out_specs = (P(), P(), P("feat", "dom"), P("feat", "dom"), P("feat", "dom"))
    return jax.shard_map(
        per_device, mesh=mesh, in_specs=in_specs, out_specs=out_specs, check_vma=False
    )
```

profile of v0, /device:TPU:0, one launch (start us, length us, event | category | flops | bytes accessed | tf_op | source)
XLA Modules:
  0.0 488.4 jit_solution(10697952890645526541)
XLA Ops:
  11.6 8.3 %all-to-all-start = ((bf16[16,2,200]{2,1,0:T(2,128)(2,1)}), bf16[16,2,200]{2,1,0:T(2,128)(2,1)S(1)}, u32[]{:S(2)}, u32[]{:S(2)}) async-start(bf16[16,2,200]{2,1,0:T(2,128)(2,1)} %reshape.262), calls=%async_computation | async-start | bytes 32768 | tf_op jit(solution)/shard_map/all_to_all | solution.py:54
  23.9 13.5 %fusion.39 = (s32[2048]{0:T(1024)S(1)}, bf16[2048,2048]{1,0:T(8,128)(2,1)S(1)}) fusion(s32[2048,2048]{1,0:T(8,128)} %param.12), kind=kLoop, calls=%fused_computation.129 | loop fusion | flops 8386560 | bytes 25174016 | tf_op jit(solution)/shard_map/reduce_sum | solution.py:128
  37.8 2.9 copy-done
  40.7 2.7 fusion.41
  43.9 89.5 %all-reduce.14.cloned.1.call-done = bf16[103680]{0:T(1024)(128)(2,1)} async-done(((bf16[103680]{0:T(1024)(128)(2,1)}), bf16[103680]{0:T(1024)(128)(2,1)}) %all-reduce.14.cloned.1.call-update) | async-done | bytes 207376
  136.7 1.9 convolution_add_fusion
  141.3 6.8 %reduce-scatter.3.cloned.1.call-done = f32[2048,128]{0,1:T(8,128)} async-done(((f32[2048,256]{0,1:T(8,128)}), f32[2048,128]{0,1:T(8,128)}) %reduce-scatter.3.cloned.1.call-update) | async-done | bytes 1048592 | tf_op jit(solution)/shard_map/reduce_scatter | solution.py:63
  148.1 1.4 fusion.35
  149.4 3.3 all-reduce.5
  152.8 1.8 multiply_convert_fusion.3
  154.6 7.5 %fusion.43 = f32[128,2048]{1,0:T(8,128)} fusion(bf16[2048,128]{0,1:T(8,128)(2,1)S(1)} %multiply_convert_fusion.3, bf16[2048,2048]{1,0:T(8,128)(2,1)} %copy-done), kind=kOutput, calls=%fused_computation.133 | convolution fusion | flops 1073741824 | bytes 9961472 | tf_op jit(solution)/shard_map/dot_general | solution.py:20
  163.8 6.9 %all-to-all-start.1 = ((bf16[16,8,128]{2,1,0:T(8,128)(2,1)}), bf16[16,8,128]{2,1,0:T(8,128)(2,1)S(1)}, u32[]{:S(2)}, u32[]{:S(2)}) async-start(bf16[16,8,128]{2,1,0:T(8,128)(2,1)} %bitcast_select_fusion.1), calls=%async_computation.2 | async-start | bytes 65536 | tf_op jit(solution)/shard_map/all_to_all | solution.py:54
  172.3 5.8 %all-to-all-done.1 = bf16[16,8,128]{2,1,0:T(8,128)(2,1)S(1)} async-done(((bf16[16,8,128]{2,1,0:T(8,128)(2,1)}), bf16[16,8,128]{2,1,0:T(8,128)(2,1)S(1)}, u32[]{:S(2)}, u32[]{:S(2)}) %all-to-all-start.1) | async-done | bytes 32800 | tf_op jit(solution)/shard_map/all_to_all | solution.py:54
  178.1 1.5 fusion.3
  180.5 2.7 convolution_add_fusion.1
  184.6 5.0 %reduce-scatter.5.cloned.1.call-done = f32[2048,128]{0,1:T(8,128)} async-done(((f32[2048,256]{0,1:T(8,128)}), f32[2048,128]{0,1:T(8,128)}) %reduce-scatter.5.cloned.1.call-update) | async-done | bytes 1048592 | tf_op jit(solution)/shard_map/reduce_scatter | solution.py:63
  190.9 3.3 all-reduce.4
  194.3 1.8 multiply_convert_fusion.2
  196.1 6.3 %fusion.45 = f32[128,2048]{1,0:T(8,128)S(1)} fusion(bf16[2048,128]{0,1:T(8,128)(2,1)S(1)} %multiply_convert_fusion.2, bf16[2048,2048]{1,0:T(8,128)(2,1)} %copy-done), kind=kOutput, calls=%fused_computation.135 | convolution fusion | flops 1073741824 | bytes 9961472 | tf_op jit(solution)/shard_map/dot_general | solution.py:20
  204.1 6.9 %all-to-all-start.2 = ((bf16[16,8,128]{2,1,0:T(8,128)(2,1)}), bf16[16,8,128]{2,1,0:T(8,128)(2,1)S(1)}, u32[]{:S(2)}, u32[]{:S(2)}) async-start(bf16[16,8,128]{2,1,0:T(8,128)(2,1)} %bitcast_select_fusion), calls=%async_computation.4 | async-start | bytes 65536 | tf_op jit(solution)/shard_map/all_to_all | solution.py:54
  211.2 7.1 %all-to-all-done.2 = bf16[16,8,128]{2,1,0:T(8,128)(2,1)S(1)} async-done(((bf16[16,8,128]{2,1,0:T(8,128)(2,1)}), bf16[16,8,128]{2,1,0:T(8,128)(2,1)S(1)}, u32[]{:S(2)}, u32[]{:S(2)}) %all-to-all-start.2) | async-done | bytes 32800 | tf_op jit(solution)/shard_map/all_to_all | solution.py:54
  220.7 15.0 %all-reduce.10.cloned.1.call-done = f32[2048,47]{0,1:T(8,128)} async-done(((f32[2048,47]{0,1:T(8,128)}), f32[2048,47]{0,1:T(8,128)}) %all-reduce.10.cloned.1.call-update) | async-done | bytes 385040 | tf_op jit(solution)/shard_map/psum | solution.py:60
  238.5 42.6 %all-reduce.1 = (f32[]{:T(128)}, f32[]{:T(128)}) all-reduce(f32[]{:T(128)} %get-tuple-element.27, f32[]{:T(128)} %get-tuple-element.26), channel_id=1, replica_groups=mesh['dom'=16,'feat'=2] {'dom'}, use_global_device_ids=true, to_apply=%region_17.19 | all-reduce | flops 2 | bytes 16 | tf_op jit(solution)/shard_map/psum | solution.py:145
  283.4 7.9 %convolution_bitcast_fusion.2 = f32[2048,128]{1,0:T(8,128)} fusion(bf16[2048,128]{1,0:T(8,128)(2,1)S(1)} %fusion.5, bf16[2048,2048]{1,0:T(8,128)(2,1)} %copy-done), kind=kOutput, calls=%fused_computation.9 | convolution fusion | flops 1073741824 | bytes 9961472 | tf_op jit(solution)/shard_map/dot_general | solution.py:24
  292.2 3.5 all-to-all-start.3
  295.8 1.6 convolution_add_fusion.2
  297.3 5.8 %all-to-all-done.3 = bf16[16,8,128]{2,1,0:T(8,128)(2,1)S(1)} async-done(((bf16[16,8,128]{2,1,0:T(8,128)(2,1)}), bf16[16,8,128]{2,1,0:T(8,128)(2,1)S(1)}, u32[]{:S(2)}, u32[]{:S(2)}) %all-to-all-start.3) | async-done | bytes 32800 | tf_op jit(solution)/shard_map/all_to_all | solution.py:102
  303.1 1.9 scatter_custom_fusion
  305.0 1.4 copy.45
  306.4 3.0 multiply_reduce_fusion
  309.3 3.4 all-reduce.3
  313.9 5.7 %all-gather.3.cloned.1.call-done = bf16[2048,256]{0,1:T(8,128)(2,1)} async-done(((bf16[2048,128]{0,1:T(8,128)(2,1)}), bf16[2048,256]{0,1:T(8,128)(2,1)}) %all-gather.3.cloned.1.call-update) | async-done | bytes 1048592 | tf_op jit(solution)/shard_map/all_gather | solution.py:163
  319.6 2.0 fusion.2
  321.6 7.8 %convolution_bitcast_fusion.1 = f32[2048,128]{1,0:T(8,128)} fusion(bf16[2048,128]{1,0:T(8,128)(2,1)S(1)} %fusion.2, bf16[2048,2048]{1,0:T(8,128)(2,1)} %copy-done), kind=kOutput, calls=%fused_computation.8 | convolution fusion | flops 1073741824 | bytes 9961472 | tf_op jit(solution)/shard_map/dot_general | solution.py:24
  330.3 6.9 %all-to-all-start.4 = ((bf16[16,8,128]{2,1,0:T(8,128)(2,1)}), bf16[16,8,128]{2,1,0:T(8,128)(2,1)S(1)}, u32[]{:S(2)}, u32[]{:S(2)}) async-start(bf16[16,8,128]{2,1,0:T(8,128)(2,1)} %fusion.10), calls=%async_computation.6 | async-start | bytes 65536 | tf_op jit(solution)/shard_map/all_to_all | solution.py:102
  337.3 2.7 convolution_add_fusion.5
  340.0 4.6 all-to-all-done.4
  344.7 3.5 scatter_custom_fusion.1
  348.1 2.6 copy.48
  350.8 3.3 multiply_reduce_fusion.1
  354.1 3.3 all-reduce.2
  357.4 2.3 multiply_convert_fusion
  362.1 1.6 convolution_bitcast_fusion.4
  364.3 1.4 all-gather.5.cloned.1.call-done
  365.7 1.8 fusion.46
  367.5 1.7 convolution_bitcast_fusion.6
  370.5 109.5 %all-reduce.12.cloned.1.call-done = f32[1,103680]{1,0:T(1,128)} async-done(((f32[1,103680]{1,0:T(1,128)}), f32[1,103680]{1,0:T(1,128)}) %all-reduce.12.cloned.1.call-update) | async-done | bytes 414736 | tf_op jit(solution)/shard_map/psum | solution.py:178
  480.0 1.6 multiply_subtract_fusion
  (154 shorter events, 37.9 us)
Async XLA Ops:
  11.6 31.8 %all-to-all-start = ((bf16[16,2,200]{2,1,0:T(2,128)(2,1)}), bf16[16,2,200]{2,1,0:T(2,128)(2,1)S(1)}, u32[]{:S(2)}, u32[]{:S(2)}) async-start(bf16[16,2,200]{2,1,0:T(2,128)(2,1)} %reshape.262), calls=%async_computation | async-start | bytes 32768 | tf_op jit(solution)/shard_map/all_to_all | solution.py:54
  19.9 113.5 %all-reduce.14.cloned.1.call-start = ((), (), s32[]{:S(2)}) async-start(), calls=%async_computation.13 | async-start | bytes 417792
  23.1 0.7 copy-start.12
  23.8 13.6 %copy-start.11 = (s32[2048,128]{1,0:T(8,128)S(1)}, s32[2048,128]{1,0:T(8,128)}, u32[]{:S(2)}) copy-start(s32[2048,128]{1,0:T(8,128)} %param.13) | copy-start | bytes 3145732
  23.8 16.8 %copy-start.8 = (bf16[2048,50]{0,1:T(8,128)(2,1)S(1)}, bf16[2048,50]{0,1:T(8,128)(2,1)}, u32[]{:S(2)}) copy-start(bf16[2048,50]{0,1:T(8,128)(2,1)} %param.11) | copy-start | bytes 614404
  23.8 124.3 %reduce-scatter.3.cloned.1.call-start = ((), (), s32[]{:S(2)}) async-start(), calls=%async_computation.7 | async-start | bytes 3145728 | tf_op jit(solution)/shard_map/reduce_scatter | solution.py:63
  37.4 3.2 copy-start
  43.3 95.3 %copy-start.16 = (s32[1,16,8]{1,2,0:T(8,128)S(1)}, s32[1,16,8]{1,2,0:T(8,128)}, u32[]{:S(2)}) copy-start(s32[1,16,8]{1,2,0:T(8,128)} %param.14) | copy-start | bytes 1540
  43.9 118.3 %copy-start.9 = (bf16[2048,50]{0,1:T(8,128)(2,1)}, bf16[2048,50]{0,1:T(8,128)(2,1)S(1)}, u32[]{:S(2)}) copy-start(bf16[2048,50]{0,1:T(8,128)(2,1)S(1)} %fusion.8) | copy-start | bytes 614404
  134.6 27.6 %copy-start.10 = (bf16[1,103680]{1,0:T(2,128)(2,1)}, bf16[1,103680]{1,0:T(2,128)(2,1)S(1)}, u32[]{:S(2)}) copy-start(bf16[1,103680]{1,0:T(2,128)(2,1)S(1)} %reshape.240) | copy-start | bytes 622084
  141.3 30.9 %copy-start.21 = (f32[128]{0:T(128)}, f32[128]{0:T(128)S(1)}, u32[]{:S(2)}) copy-start(f32[128]{0:T(128)S(1)} %get-tuple-element.54) | copy-start | bytes 1540
  154.6 28.6 %copy-start.4 = (bf16[2048,128]{0,1:T(8,128)(2,1)}, bf16[2048,128]{0,1:T(8,128)(2,1)S(1)}, u32[]{:S(2)}) copy-start(bf16[2048,128]{0,1:T(8,128)(2,1)S(1)} %multiply_convert_fusion.3) | copy-start | bytes 1572868
  162.4 31.8 %copy-start.23 = (f32[128]{0:T(128)S(1)}, f32[128]{0:T(128)}, u32[]{:S(2)}) copy-start(f32[128]{0:T(128)} %get-tuple-element.53) | copy-start | bytes 1540
  163.8 14.3 %all-to-all-start.1 = ((bf16[16,8,128]{2,1,0:T(8,128)(2,1)}), bf16[16,8,128]{2,1,0:T(8,128)(2,1)S(1)}, u32[]{:S(2)}, u32[]{:S(2)}) async-start(bf16[16,8,128]{2,1,0:T(8,128)(2,1)} %bitcast_select_fusion.1), calls=%async_computation.2 | async-start | bytes 65536 | tf_op jit(solution)/shard_map/all_to_all | solution.py:54
  170.7 18.8 %reduce-scatter.5.cloned.1.call-start = ((), (), s32[]{:S(2)}) async-start(), calls=%async_computation.8 | async-start | bytes 3145728 | tf_op jit(solution)/shard_map/reduce_scatter | solution.py:63
  179.7 0.8 copy-start.6
  196.1 40.7 %copy-start.17 = (s32[2048]{0:T(1024)S(1)}, s32[2048]{0:T(1024)}, u32[]{:S(2)}) copy-start(s32[2048]{0:T(1024)} %param.15) | copy-start | bytes 24580
  196.1 41.8 %copy-start.18 = (s32[2048]{0:T(1024)S(1)}, s32[2048]{0:T(1024)}, u32[]{:S(2)}) copy-start(s32[2048]{0:T(1024)} %param.16) | copy-start | bytes 24580
  204.1 14.3 %all-to-all-start.2 = ((bf16[16,8,128]{2,1,0:T(8,128)(2,1)}), bf16[16,8,128]{2,1,0:T(8,128)(2,1)S(1)}, u32[]{:S(2)}, u32[]{:S(2)}) async-start(bf16[16,8,128]{2,1,0:T(8,128)(2,1)} %bitcast_select_fusion), calls=%async_computation.4 | async-start | bytes 65536 | tf_op jit(solution)/shard_map/all_to_all | solution.py:54
  210.9 24.8 %all-reduce.10.cloned.1.call-start = ((), (), s32[]{:S(2)}) async-start(), calls=%async_computation.9 | async-start | bytes 786432 | tf_op jit(solution)/shard_map/psum | solution.py:60
  218.7 0.8 copy-start.7
  220.7 84.3 %copy-start.27 = (s32[128]{0:T(128)}, s32[128]{0:T(128)S(1)}, u32[]{:S(2)}) copy-start(s32[128]{0:T(128)S(1)} %fusion.33) | copy-start | bytes 1540
  283.3 23.0 %copy-start.3 = (f32[2048,128]{0,1:T(8,128)S(1)}, f32[2048,128]{0,1:T(8,128)}, u32[]{:S(2)}) copy-start(f32[2048,128]{0,1:T(8,128)} %reduce-scatter.5.cloned.1.call-done) | copy-start | bytes 3145732
  283.3 23.0 %copy-start.24 = (f32[128]{0:T(128)S(1)}, f32[128]{0:T(128)}, u32[]{:S(2)}) copy-start(f32[128]{0:T(128)} %get-tuple-element.53) | copy-start | bytes 1540
  291.3 28.3 %copy-start.13 = (bf16[128,256]{1,0:T(8,128)(2,1)S(1)}, bf16[128,256]{1,0:T(8,128)(2,1)}, u32[]{:S(2)}) copy-start(bf16[128,256]{1,0:T(8,128)(2,1)} %squeeze.29) | copy-start | bytes 196612
  292.2 10.9 %all-to-all-start.3 = ((bf16[16,8,128]{2,1,0:T(8,128)(2,1)}), bf16[16,8,128]{2,1,0:T(8,128)(2,1)S(1)}, u32[]{:S(2)}, u32[]{:S(2)}) async-start(bf16[16,8,128]{2,1,0:T(8,128)(2,1)} %fusion.9), calls=%async_computation.5 | async-start | bytes 65536 | tf_op jit(solution)/shard_map/all_to_all | solution.py:102
  295.7 23.9 %all-gather.3.cloned.1.call-start = ((), (), s32[]{:S(2)}) async-start(), calls=%async_computation.10 | async-start | bytes 1572864 | tf_op jit(solution)/shard_map/all_gather | solution.py:163
  309.3 28.0 %copy-start.14 = (bf16[128,256]{1,0:T(8,128)(2,1)S(1)}, bf16[128,256]{1,0:T(8,128)(2,1)}, u32[]{:S(2)}) copy-start(bf16[128,256]{1,0:T(8,128)(2,1)} %squeeze.28) | copy-start | bytes 196612
  319.6 17.7 %copy-start.1 = (bf16[2048,256]{0,1:T(8,128)(2,1)S(1)}, bf16[2048,256]{0,1:T(8,128)(2,1)}, u32[]{:S(2)}) copy-start(bf16[2048,256]{0,1:T(8,128)(2,1)} %all-gather.3.cloned.1.call-done) | copy-start | bytes 3145732
  321.5 29.2 %copy-start.2 = (f32[2048,128]{0,1:T(8,128)S(1)}, f32[2048,128]{0,1:T(8,128)}, u32[]{:S(2)}) copy-start(f32[2048,128]{0,1:T(8,128)} %reduce-scatter.3.cloned.1.call-done) | copy-start | bytes 3145732
  321.6 29.2 %copy-start.22 = (f32[128]{0:T(128)S(1)}, f32[128]{0:T(128)}, u32[]{:S(2)}) copy-start(f32[128]{0:T(128)} %copy-done.21) | copy-start | bytes 1540
  330.3 33.4 %copy-start.5 = (bf16[2048,128]{0,1:T(8,128)(2,1)S(1)}, bf16[2048,128]{0,1:T(8,128)(2,1)}, u32[]{:S(2)}) copy-start(bf16[2048,128]{0,1:T(8,128)(2,1)} %copy-done.4) | copy-start | bytes 1572868
  330.3 14.3 %all-to-all-start.4 = ((bf16[16,8,128]{2,1,0:T(8,128)(2,1)}), bf16[16,8,128]{2,1,0:T(8,128)(2,1)S(1)}, u32[]{:S(2)}, u32[]{:S(2)}) async-start(bf16[16,8,128]{2,1,0:T(8,128)(2,1)} %fusion.10), calls=%async_computation.6 | async-start | bytes 65536 | tf_op jit(solution)/shard_map/all_to_all | solution.py:102
  337.3 28.4 %all-gather.5.cloned.1.call-start = ((), (), s32[]{:S(2)}) async-start(), calls=%async_computation.11 | async-start | bytes 1572864 | tf_op jit(solution)/shard_map/all_gather | solution.py:163
  350.7 18.6 %copy-start.26 = (f32[128]{0:T(128)S(1)}, f32[128]{0:T(128)}, u32[]{:S(2)}) copy-start(f32[128]{0:T(128)} %get-tuple-element.6) | copy-start | bytes 1540
  350.7 18.6 %copy-start.25 = (f32[128]{0:T(128)S(1)}, f32[128]{0:T(128)}, u32[]{:S(2)}) copy-start(f32[128]{0:T(128)} %get-tuple-element.12) | copy-start | bytes 1540
  350.8 129.2 %copy-start.15 = (f32[1,6480]{1,0:T(1,128)S(1)}, f32[1,6480]{1,0:T(1,128)}, u32[]{:S(2)}) copy-start(f32[1,6480]{1,0:T(1,128)} %param.17) | copy-start | bytes 77764
  350.8 129.2 %copy-start.19 = (f32[1,6480]{1,0:T(1,128)S(1)}, f32[1,6480]{1,0:T(1,128)}, u32[]{:S(2)}) copy-start(f32[1,6480]{1,0:T(1,128)} %param.18) | copy-start | bytes 77764
  350.8 129.2 %copy-start.20 = (f32[1,6480]{1,0:T(1,128)S(1)}, f32[1,6480]{1,0:T(1,128)}, u32[]{:S(2)}) copy-start(f32[1,6480]{1,0:T(1,128)} %param.19) | copy-start | bytes 77764
  359.8 120.2 %all-reduce.12.cloned.1.call-start = ((), (), s32[]{:S(2)}) async-start(), calls=%async_computation.12 | async-start | bytes 829440 | tf_op jit(solution)/shard_map/psum | solution.py:178
Sparse Core Ops, SparseCore 0:
  26.0 107.3 all-reduce.13
  138.7 9.3 reduce-scatter.2
  183.4 6.1 reduce-scatter.4
  220.6 15.0 all-reduce.9
  314.0 5.5 all-gather.2
  359.9 5.7 all-gather.4
  370.9 109.0 all-reduce.11
where the time goes:
time: 490 us; the launch traced here: 488 us
  waiting for transfers between devices  256 us (52%)
  matrix products  57.9 us (12%)
  blocking collectives  56 us (11%)
  other arithmetic  45.1 us (9%)
  starting transfers between devices  33.2 us (7%)
  local copies, waits for them, and re-layouts  24.5 us (5%)
  between operations  15.5 us (3%)
    psum x1, waiting for transfers between devices, per_device(): summed_all = lax.psum(gradient, 'dom')  109 us
    unnamed x8, waiting for transfers between devices  89.6 us
    psum x1, blocking collectives, per_device(): lax.psum((jnp.sum((log_total - picked) * weight_mask), jnp.sum(weight_mas...  42.6 us
    dot_general x12, matrix products, product(): return jnp.dot(matrix_a, matrix_b, preferred_element_type=jnp.float32)  26.4 us
    dot_general x10, matrix products, contract_rows(): lax.dot_general(matrix_a, matrix_b, (((0,), (0,)), ((), ())), preferred_e...  24.8 us
    all_to_all x3, starting transfers between devices, layer_forward(): lax.all_to_all(outgoing, 'dom', split_axis=0, concat_axis=0, tiled=True)  22 us
    psum x1, waiting for transfers between devices, layer_forward(): mixed = lax.psum(partial_value, 'feat')  15 us
    reduce_sum x2, other arithmetic, per_device(): degree = jnp.sum(local_mask, axis=1) + jnp.sum(halo_mask, axis=1)  13.9 us
  transfers between devices with their start and end apart: 12, of which 11 were waited for; matrix products, arithmetic and copies ran while one was open for 7% of the time, Pallas kernels for 0%

commit v1 on v0

v1 whole, which is shorter than its diff:
```python
import functools

import jax
import jax.numpy as jnp
from jax import lax
from jax.experimental import pallas as pl
from jax.experimental.pallas import tpu as pltpu
from jax.sharding import PartitionSpec as P

HID = 256
CLS = 47
STEP = 10
EPSILON = 1e-05
LEARN_RATE = 0.02
DECAY_ONE = 0.9
DECAY_TWO = 0.999
ADAM_EPS = 1e-08
WEIGHT_DECAY = 0.01

MESH = pl.DeviceIdType.MESH
BF = jnp.bfloat16
F32 = jnp.float32
LANES = 128
CLS_PAD = 64
FEAT_PAD = 64
HALF_HID = HID // 2
ROW_ONE = 2 * FEAT_PAD
ROW_TWO = ROW_ONE + 2 * HALF_HID
HEAD_ROWS = 2 * HALF_HID * CLS // HID
ROW_NORM = ROW_TWO + 48
ROWS_PAD = ROW_NORM + 16
GELU_A = 0.7978845608028654
GELU_B = 0.044715


def dot(a, b, ca=1, cb=0, precision=None):
    return lax.dot_general(
        a, b, (((ca,), (cb,)), ((), ())), precision=precision, preferred_element_type=F32
    )


def iota(shape, axis):
    return lax.broadcasted_iota(jnp.int32, shape, axis)


def gelu(x):
    t = jnp.tanh(GELU_A * (x + GELU_B * (x * x * x)))
    return 0.5 * x * (1.0 + t)


def gelu_grad(x):
    xx = x * x
    t = jnp.tanh(GELU_A * (x + GELU_B * (xx * x)))
    return 0.5 * (1.0 + t) + 0.5 * x * (1.0 - t * t) * (GELU_A + (3.0 * GELU_A * GELU_B) * xx)


def roll_rows(x, amount, right):
    for bit in range(8):
        step = 1 << bit
        moved = pltpu.roll(x, step if right else HID - step, 1)
        x = jnp.where((amount & step) != 0, moved, x)
    return x


def loop(n, body):
    def step(i, carry):
        body(i)
        return carry

    lax.fori_loop(0, n, step, 0)


def kernel(
    cfg,
    x_in, lm_in, hm_in, send_in, label_in, lmask_in, master_in,
    grad_out, scalar_out,
    a_stage, b_stage, h_stage, x_stage, x_pad,
    a_rows, b_x, hmt, sel, xs, hs, gs_all, agg_ref, agg_zero,
    mixed, normed, scale_inv, inv_ref, halo_tx, halo_rx,
    flat_t, par_tx, par_rx, wmat, wmat_t, norm_col, head_ws, head_wn, head_ws_t, head_wn_t,
    g_low, grad_a, grad_b, grad_flat, pair_rx, win_tx, win_rx, dw_head, acc_gain, acc_bias, loss_ref,
    local_sem, pair_send, pair_recv, halo_send, halo_recv, par_send, par_recv, win_send, win_recv,
):
    n_dom, nodes, half, halo, shard, fin = (
        cfg["n_dom"], cfg["nodes"], cfg["half"], cfg["halo"], cfg["shard"], cfg["fin"]
    )
    win, par_rows, rows_all = cfg["win"], cfg["par_rows"], cfg["rows_all"]
    me, f = lax.axis_index("dom"), lax.axis_index("feat")
    other = 1 - f
    own = pl.multiple_of(f * half, half)
    far = pl.multiple_of(other * half, half)
    own_cols, far_cols = pl.ds(own, half), pl.ds(far, half)

    chunk = 128
    n_chunk = half // chunk
    x_copy = pltpu.make_async_copy(x_in, x_stage, local_sem.at[0])
    x_copy.start()
    h_rows = cfg["h_rows"]

    def h_copy(i):
        return pltpu.make_async_copy(
            hm_in.at[pl.ds(i * h_rows, h_rows), :], h_stage, local_sem.at[1]
        )

    h_copy(0).start()

    def a_copy(i):
        return pltpu.make_async_copy(
            lm_in.at[pl.ds(pl.multiple_of(own + i * chunk, chunk), chunk), :],
            a_stage.at[pl.ds(pl.multiple_of(i * chunk, chunk), chunk), :],
            local_sem.at[2 + i],
        )

    for i in range(n_chunk):
        a_copy(i).start()
    b_copy = pltpu.make_async_copy(
        lm_in.at[far_cols, own_cols], b_stage, local_sem.at[2 + n_chunk]
    )
    b_copy.start()

    barrier = pltpu.get_barrier_semaphore()

    def greet(i):
        p = lax.rem(me + i + 1, n_dom)
        pl.semaphore_signal(barrier, inc=1, device_id=(p, f), device_id_type=MESH)

    loop(n_dom - 1, greet)
    pl.semaphore_signal(barrier, inc=1, device_id=(me, other), device_id_type=MESH)

    def pair_copy(src, dst, k):
        return pltpu.make_async_remote_copy(
            src_ref=src, dst_ref=dst, send_sem=pair_send.at[k], recv_sem=pair_recv.at[k],
            device_id=(me, other), device_id_type=MESH,
        )

    off = lax.rem(shard * me, HID)
    off_row, off_lane = off // LANES, lax.rem(off, LANES)
    t_rows = 2 * win
    lane_t = iota((t_rows, LANES), 1)

    def to_window(t):
        r = pltpu.roll(t, off_lane, 1)
        t = jnp.where(lane_t < off_lane, pltpu.roll(r, 1, 0), r)
        t = jnp.where(off_row == 1, pltpu.roll(t, 1, 0), t)
        flat_t[...] = t
        return jnp.concatenate(
            [flat_t[pl.ds(0, win, stride=2), :], flat_t[pl.ds(1, win, stride=2), :]], axis=1
        )

    def from_window(w):
        flat_t[pl.ds(0, win, stride=2), :] = w[:, :LANES]
        flat_t[pl.ds(1, win, stride=2), :] = w[:, LANES:]
        t = flat_t[...]
        t = jnp.where(off_row == 1, pltpu.roll(t, t_rows - 1, 0), t)
        back = lax.rem(LANES - off_lane, LANES)
        near = pltpu.roll(t, back, 1)
        after = pltpu.roll(near, t_rows - 1, 0)
        return jnp.where(lane_t + off_lane < LANES, near, after)

    flat_t[...] = jnp.zeros_like(flat_t)
    for k in range(-(-shard // LANES)):
        width = min(LANES, shard - k * LANES)
        flat_t[k : k + 1, 0:width] = master_in[0:1, k * LANES : k * LANES + width]
    window = to_window(flat_t[...])
    if par_rows > win:
        window = jnp.concatenate([window, jnp.zeros((par_rows - win, HID), F32)], axis=0)
    par_tx[...] = window.astype(BF)
    par_rx[f, pl.ds(pl.multiple_of(me * par_rows, par_rows), par_rows), :] = par_tx[...]

    x_copy.wait()
    pad_rows = iota((FEAT_PAD, nodes), 0)
    x_pad[...] = jnp.where(pad_rows == fin, 1.0, 0.0)
    x_pad[0:fin, :] = x_stage[...].astype(F32)
    xs[pl.ds(pl.multiple_of(f * FEAT_PAD, FEAT_PAD), FEAT_PAD), :] = x_pad[...].astype(BF)

    pl.semaphore_wait(barrier, n_dom)

    slice_rows = pl.ds(pl.multiple_of(f * FEAT_PAD, FEAT_PAD), FEAT_PAD)
    x_pair = pair_copy(xs.at[slice_rows, :], xs.at[slice_rows, :], 0)
    x_pair.start()

    def par_copy(p):
        return pltpu.make_async_remote_copy(
            src_ref=par_tx,
            dst_ref=par_rx.at[f, pl.ds(pl.multiple_of(me * par_rows, par_rows), par_rows), :],
            send_sem=par_send, recv_sem=par_recv, device_id=(p, f), device_id_type=MESH,
        )

    loop(n_dom - 1, lambda i: par_copy(lax.rem(me + i + 1, n_dom)).start())

    send_rows = send_in[...].astype(F32)
    lane_d = iota(send_rows.shape, 1)
    node_lane = iota((16, nodes), 1).astype(F32)

    def build_sel(q):
        first = jnp.sum(jnp.where(lane_d == 2 * q, send_rows, 0.0), axis=1, keepdims=True)
        second = jnp.sum(jnp.where(lane_d == 2 * q + 1, send_rows, 0.0), axis=1, keepdims=True)
        rows = jnp.concatenate([first, second], axis=0)
        sel[pl.ds(pl.multiple_of(q * 16, 16), 16), :] = jnp.where(
            node_lane == rows, 1.0, 0.0
        ).astype(BF)

    loop(n_dom // 2, build_sel)

    def halo_copy(k, p):
        return pltpu.make_async_remote_copy(
            src_ref=halo_tx.at[k, p], dst_ref=halo_rx.at[k, me],
            send_sem=halo_send.at[k], recv_sem=halo_recv.at[k],
            device_id=(p, f), device_id_type=MESH,
        )

    def send_halo(k):
        loop(n_dom - 1, lambda i: halo_copy(k, lax.rem(me + i + 1, n_dom)).start())
        halo_rx[k, me] = halo_tx[k, me]

    def pack_halo(k, rows):
        v = rows.reshape(n_dom, 8, HID)
        halo_tx[k] = jnp.concatenate([v[:, :, :LANES], v[:, :, LANES:]], axis=1).astype(BF)

    def wait_halo(k):
        part = pl.ds(0, n_dom - 1)
        pltpu.make_async_copy(halo_rx.at[k, part], halo_rx.at[k, part], halo_recv.at[k]).wait()

    def wait_halo_sent(k):
        part = pl.ds(0, n_dom - 1)
        pltpu.make_async_copy(halo_tx.at[k, part], halo_tx.at[k, part], halo_send.at[k]).wait()

    def read_halo(k):
        v = halo_rx[k].astype(F32)
        rows = jnp.concatenate(
            [v[:, :8, :].reshape(halo, LANES), v[:, 8:, :].reshape(halo, LANES)], axis=1
        )
        return rows.T.astype(BF)

    x_pair.wait_recv()
    picked = dot(sel[...], xs[...], 1, 1).reshape(n_dom, 8, LANES)
    count = jnp.sum(lmask_in[...].astype(F32), axis=1, keepdims=True)
    count_high = jnp.floor(count * (1.0 / 256.0))
    count_low = count - 256.0 * count_high
    count_row = iota((8, LANES), 0)
    counts = jnp.where(count_row == 0, count_high, jnp.where(count_row == 1, count_low, 0.0))
    counts = jnp.broadcast_to(counts[None], (n_dom, 8, LANES))
    halo_tx[0] = jnp.concatenate([picked, counts], axis=1).astype(BF)
    send_halo(0)

    for i in range(nodes // h_rows):
        h_copy(i).wait()
        hmt[:, i * h_rows : (i + 1) * h_rows] = h_stage[...].astype(F32).T.astype(BF)
        if (i + 1) * h_rows < nodes:
            h_copy(i + 1).start()

    def convert_a(i):
        a_copy(i).wait()
        rows = pl.ds(pl.multiple_of(i * chunk, chunk), chunk)
        a_rows[rows, :] = a_stage[rows, :].astype(F32).astype(BF)

    loop(n_chunk, convert_a)
    b_copy.wait()
    b_x[...] = b_stage[...].astype(F32).astype(BF)

    part = pl.ds(0, (n_dom - 1) * par_rows)
    pltpu.make_async_copy(par_rx.at[f, part, :], par_rx.at[f, part, :], par_recv).wait()
    par_pair = pair_copy(par_rx.at[f], par_rx.at[f], 1)
    par_pair.start()

    agg_zero[...] = dot(xs[...], a_rows[...], 1, 1)
    wait_halo(0)
    arrived = halo_rx[0].astype(F32)
    halo_zero = arrived[:, :8, :].reshape(halo, LANES).T.astype(BF)
    count_all = jnp.sum(arrived[:, 8:, :], axis=0)
    label_count = 256.0 * count_all[0:1, 0:1] + count_all[1:2, 0:1]
    summed = agg_zero[...] + dot(halo_zero, hmt[:, own_cols])
    inverse = 1.0 / jnp.maximum(summed[fin : fin + 1, :], 1.0)
    inv_ref[...] = jnp.broadcast_to(inverse, inv_ref.shape)
    agg_ref[2, 0:LANES, :] = (summed * inverse).astype(BF)

    par_pair.wait_recv()
    k_all = n_dom * par_rows
    r_pad = iota((ROWS_PAD, k_all), 0)
    k_col = iota((ROWS_PAD, k_all), 1)
    owner, inner = k_col // par_rows, lax.rem(k_col, par_rows)
    target = lax.shift_right_logical(owner * shard, 8) + inner
    row_of = jnp.where(
        r_pad < fin, r_pad,
        jnp.where(
            (r_pad >= FEAT_PAD) & (r_pad < FEAT_PAD + fin), r_pad - (FEAT_PAD - fin),
            jnp.where(
                (r_pad >= ROW_ONE) & (r_pad < ROW_TWO + HEAD_ROWS), r_pad - (ROW_ONE - 2 * fin),
                jnp.where(
                    (r_pad >= ROW_NORM) & (r_pad < ROW_NORM + 2),
                    r_pad - ROW_NORM + (rows_all - 2), -1,
                ),
            ),
        ),
    )
    place = jnp.where(row_of == target, 1.0, 0.0).astype(BF)
    node = iota((HID, 48), 0)
    first_row = lax.shift_right_logical(node * CLS, 8)
    row_id = iota((HID, 48), 1)
    pick_a = jnp.where(row_id == first_row, 1.0, 0.0)
    pick_b = jnp.where(row_id == first_row + 1, 1.0, 0.0)
    start_lane = (iota((HID, HID), 0) * CLS) & (HID - 1)
    lane_w = iota((HID, HID), 1)
    for c in range(2):
        rows = dot(place, par_rx[c])
        rows_t = rows.T
        wmat[c] = rows.astype(BF)
        wmat_t[c] = rows_t.astype(BF)
        for k in range(2):
            col = rows_t[:, ROW_NORM + k : ROW_NORM + k + 1]
            norm_col[c * HALF_HID : (c + 1) * HALF_HID, 2 * k : 2 * k + 1] = col[:HALF_HID]
            norm_col[c * HALF_HID : (c + 1) * HALF_HID, 2 * k + 1 : 2 * k + 2] = col[HALF_HID:]
        flat = rows[ROW_TWO : ROW_TWO + 48].astype(BF)
        lo, hi = dot(pick_a.astype(BF), flat), dot(pick_b.astype(BF), flat)
        wide = jnp.where(lane_w >= start_lane, lo, hi)
        wide = roll_rows(wide, start_lane, False)
        head = jnp.where(lane_w < CLS, wide, 0.0)[:, :LANES]
        head_t = head.T[:CLS_PAD]
        half_rows = slice(c * HALF_HID, (c + 1) * HALF_HID)
        head_ws[half_rows, :] = head[:HALF_HID].astype(BF)
        head_wn[half_rows, :] = head[HALF_HID:].astype(BF)
        head_ws_t[:, half_rows] = head_t[:, :HALF_HID].astype(BF)
        head_wn_t[:, half_rows] = head_t[:, HALF_HID:].astype(BF)

    wide_cols = 128
    n_cols = half // wide_cols

    def norm_forward(layer, dest):
        def body(j):
            cols = pl.ds(pl.multiple_of(j * wide_cols, wide_cols), wide_cols)
            x = mixed[:, cols]
            centre = x - jnp.mean(x, axis=0, keepdims=True)
            rs = lax.rsqrt(jnp.mean(centre * centre, axis=0, keepdims=True) + EPSILON)
            n = centre * rs
            normed[layer, :, cols] = n
            scale_inv[layer, :, cols] = jnp.broadcast_to(rs, (8, wide_cols))
            shifted = n * norm_col[:, 2 * layer : 2 * layer + 1] + norm_col[
                :, 2 * layer + 1 : 2 * layer + 2
            ]
            out = pl.ds(pl.multiple_of(own + j * wide_cols, wide_cols), wide_cols)
            hs[dest, :, out] = gelu(shifted).astype(BF)

        loop(n_cols, body)

    x_own = xs[:, own_cols]
    agg_own = agg_ref[2, 0:LANES, :]
    states = jnp.concatenate(
        [x_own[:FEAT_PAD], agg_own[:FEAT_PAD], x_own[FEAT_PAD:], agg_own[FEAT_PAD:]], axis=0
    )
    w_zero = jnp.concatenate([wmat_t[0, :, :ROW_ONE], wmat_t[1, :, :ROW_ONE]], axis=1)
    mixed[...] = dot(w_zero, states)
    norm_forward(0, 0)

    def exchange_forward(k):
        copy = pair_copy(hs.at[k, :, own_cols], hs.at[k, :, own_cols], 2 + k)
        copy.start()
        copy.wait_recv()
        pack_halo(1 + k, dot(sel[...], hs[k], 1, 1))
        send_halo(1 + k)
        return copy

    def aggregate(k):
        mixed[...] = dot(hs[k], a_rows[...], 1, 1)
        wait_halo(1 + k)
        total = mixed[...] + dot(read_halo(1 + k), hmt[:, own_cols])
        agg_ref[k] = (total * inv_ref[0:1, :]).astype(BF)

    h_pair_one = exchange_forward(0)
    aggregate(0)
    w_self_t = jnp.concatenate(
        [wmat_t[0, :, ROW_ONE : ROW_ONE + LANES], wmat_t[1, :, ROW_ONE : ROW_ONE + LANES]], axis=1
    )
    w_neigh_t = jnp.concatenate(
        [wmat_t[0, :, ROW_ONE + LANES : ROW_TWO], wmat_t[1, :, ROW_ONE + LANES : ROW_TWO]], axis=1
    )
    mixed[...] = dot(w_self_t, hs[0, :, own_cols]) + dot(w_neigh_t, agg_ref[0])
    norm_forward(1, 1)
    h_pair_two = exchange_forward(1)
    aggregate(1)

    logits = dot(head_ws_t[...], hs[1, :, own_cols]) + dot(head_wn_t[...], agg_ref[1])
    class_id = iota((CLS_PAD, half), 0)
    logits = jnp.where(class_id < CLS, logits, -1e30)
    top = jnp.max(logits, axis=0, keepdims=True)
    log_total = top + jnp.log(jnp.sum(jnp.exp(logits - top), axis=0, keepdims=True))
    onehot = class_id == label_in[0:1, own_cols]
    weight = lmask_in[0:1, own_cols].astype(F32)
    chosen = jnp.sum(jnp.where(onehot, logits, 0.0), axis=0, keepdims=True)
    loss_part = jnp.sum((log_total - chosen) * weight, axis=1, keepdims=True)
    loss_ref[...] = jnp.broadcast_to(loss_part, loss_ref.shape)
    probs = jnp.exp(logits - log_total)
    g_logits = (probs - jnp.where(onehot, 1.0, 0.0)) * (weight / label_count)
    g_low[0, 0:CLS_PAD, :] = g_logits.astype(BF)
    g_head = g_low[0, 0:CLS_PAD, :]

    def exchange_backward(k):
        copy = pair_copy(gs_all.at[k, :, own_cols], gs_all.at[k, :, own_cols], 4 + k)
        copy.start()
        copy.wait_recv()
        pack_halo(3 + k, dot(hmt[...], gs_all[k], 1, 1))
        send_halo(3 + k)
        return copy

    def spread(k):
        mixed[...] += dot(gs_all[k, :, own_cols], a_rows[:, own_cols]) + dot(
            gs_all[k, :, far_cols], b_x[...]
        )
        wait_halo(3 + k)
        mixed[...] += dot(read_halo(3 + k), sel[:, own_cols])

    def norm_backward(layer, dest):
        acc_gain[...] = jnp.zeros_like(acc_gain)
        acc_bias[...] = jnp.zeros_like(acc_bias)

        def body(j):
            cols = pl.ds(pl.multiple_of(j * wide_cols, wide_cols), wide_cols)
            n = normed[layer, :, cols]
            gain = norm_col[:, 2 * layer : 2 * layer + 1]
            shifted = n * gain + norm_col[:, 2 * layer + 1 : 2 * layer + 2]
            g_shift = mixed[:, cols] * gelu_grad(shifted)
            acc_gain[...] += g_shift * n
            acc_bias[...] += g_shift
            gn = g_shift * gain
            mean_one = jnp.mean(gn, axis=0, keepdims=True)
            mean_two = jnp.mean(gn * n, axis=0, keepdims=True)
            g_mixed = (gn - mean_one - n * mean_two) * scale_inv[layer, 0:1, cols]
            g_low[dest, :, cols] = g_mixed.astype(BF)

        loop(n_cols, body)
        gain_row = jnp.sum(acc_gain[...].T, axis=0, keepdims=True)
        bias_row = jnp.sum(acc_bias[...].T, axis=0, keepdims=True)
        base = rows_all - 2 + layer
        for ref, c in ((grad_a, 0), (grad_b, 1)):
            piece = slice(c * HALF_HID, (c + 1) * HALF_HID)
            ref[base : base + 1, :LANES] = gain_row[:, piece]
            ref[base : base + 1, LANES:] = bias_row[:, piece]

    gs_all[0, :, own_cols] = (dot(head_wn[:, :CLS_PAD], g_head) * inv_ref[0:1, :]).astype(BF)
    g_pair_two = exchange_backward(0)
    mixed[...] = dot(head_ws[:, :CLS_PAD], g_head)
    lane_h = iota((HID, HID), 1)
    dws = dot(hs[1, :, own_cols], g_head, 1, 1)
    dwn = dot(agg_ref[1], g_head, 1, 1)
    for ref, c in ((grad_a, 0), (grad_b, 1)):
        piece = slice(c * HALF_HID, (c + 1) * HALF_HID)
        dw_head[...] = jnp.zeros_like(dw_head)
        dw_head[:HALF_HID, :CLS_PAD] = dws[piece]
        dw_head[HALF_HID:, :CLS_PAD] = dwn[piece]
        wide = roll_rows(dw_head[...], start_lane, True)
        low_part = jnp.where(lane_h >= start_lane, wide, 0.0)
        high_part = jnp.where(lane_h >= start_lane, 0.0, wide)
        flat = dot(pick_a, low_part, 0, 0, lax.Precision.HIGHEST) + dot(
            pick_b, high_part, 0, 0, lax.Precision.HIGHEST
        )
        base = 2 * fin + 2 * HALF_HID
        ref[base : base + HEAD_ROWS, :] = flat[:HEAD_ROWS]
    spread(0)
    norm_backward(1, 1)

    g_one = g_low[1]
    w_self = jnp.concatenate(
        [wmat[0, ROW_ONE : ROW_ONE + LANES], wmat[1, ROW_ONE : ROW_ONE + LANES]], axis=0
    )
    w_neigh = jnp.concatenate(
        [wmat[0, ROW_ONE + LANES : ROW_TWO], wmat[1, ROW_ONE + LANES : ROW_TWO]], axis=0
    )
    gs_all[1, :, own_cols] = (dot(w_neigh, g_one) * inv_ref[0:1, :]).astype(BF)
    g_pair_one = exchange_backward(1)
    mixed[...] = dot(w_self, g_one)
    dws = dot(hs[0, :, own_cols], g_one, 1, 1)
    dwn = dot(agg_ref[0], g_one, 1, 1)
    for ref, c in ((grad_a, 0), (grad_b, 1)):
        piece = slice(c * HALF_HID, (c + 1) * HALF_HID)
        base = 2 * fin
        ref[base : base + HALF_HID, :] = dws[piece]
        ref[base + HALF_HID : base + 2 * HALF_HID, :] = dwn[piece]
    spread(1)
    norm_backward(0, 2)

    g_zero = g_low[2]
    dws = dot(x_own, g_zero, 1, 1)
    dwn = dot(agg_own, g_zero, 1, 1)
    for ref, c in ((grad_a, 0), (grad_b, 1)):
        start = c * FEAT_PAD
        ref[0:fin, :] = dws[start : start + fin]
        ref[fin : 2 * fin, :] = dwn[start : start + fin]
        tail = ref.shape[0] - 8
        ref[tail : tail + 8, :] = jnp.broadcast_to(loss_ref[:, 0:1], (8, HID))

    @pl.when(f == 0)
    def _():
        grad_flat[0] = grad_a[...]
        grad_flat[1] = grad_b[...]

    @pl.when(f == 1)
    def _():
        grad_flat[0] = grad_b[...]
        grad_flat[1] = grad_a[...]

    grad_pair = pair_copy(grad_flat.at[1], pair_rx, 6)
    grad_pair.start()
    grad_pair.wait_recv()
    grad_a[...] = grad_flat[0] + pair_rx[...]
    tail = cfg["grad_rows"] - 8

    def window_of(d):
        start = lax.shift_right_logical(shard * d, 8)
        shift = start & 7
        base = pl.multiple_of(start - shift, 8)
        rows = pltpu.roll(grad_a[pl.ds(base, win + 8), :], win + 8 - shift, 0)[:win]
        last = iota((win, HID), 0) == win - 1
        return jnp.where(last, grad_a[tail : tail + 1, :], rows)

    def win_copy(p):
        return pltpu.make_async_remote_copy(
            src_ref=win_tx.at[p], dst_ref=win_rx.at[me],
            send_sem=win_send, recv_sem=win_recv, device_id=(p, f), device_id_type=MESH,
        )

    def send_window(i):
        p = lax.rem(me + i + 1, n_dom)
        win_tx[p] = window_of(p)
        win_copy(p).start()

    loop(n_dom - 1, send_window)
    win_rx[me] = window_of(me)
    part = pl.ds(0, n_dom - 1)
    pltpu.make_async_copy(win_rx.at[part], win_rx.at[part], win_recv).wait()
    total = jnp.sum(win_rx[...], axis=0)
    scalar_out[0:1, :] = total[win - 1 : win, :LANES]
    scalar_out[1:2, :] = jnp.broadcast_to(label_count, (1, LANES))
    total = jnp.where(iota((win, HID), 0) == win - 1, 0.0, total)
    grad_out[...] = from_window(total)

    for copy in (x_pair, par_pair, h_pair_one, h_pair_two, g_pair_two, g_pair_one, grad_pair):
        copy.wait_send()
    for k in range(5):
        wait_halo_sent(k)
    pltpu.make_async_copy(win_tx.at[part], win_tx.at[part], win_send).wait()
    part = pl.ds(0, (n_dom - 1) * par_rows)
    pltpu.make_async_copy(par_rx.at[f, part, :], par_rx.at[f, part, :], par_send).wait()


def round_up(value, step):
    return -(-value // step) * step


def per_device(n_dom, features, local_mask, halo_mask, send_rows, labels, label_mask, master, first, second):
    nodes, halo = local_mask.shape[1], halo_mask.shape[1]
    half, shard, fin = nodes // 2, master.shape[1], features.shape[1]
    rows_all = n_dom * shard // HID
    span = (shard + HID - 2) // HID + 1
    win = round_up(span + 1, 8)
    par_rows = round_up(span, 16)
    grad_rows = round_up(rows_all + win, 8) + 8
    cfg = dict(
        n_dom=n_dom, nodes=nodes, half=half, halo=halo, shard=shard, fin=fin, win=win,
        par_rows=par_rows, rows_all=rows_all, grad_rows=grad_rows,
        h_rows=min(nodes, 2**18 // halo),
    )
    hbm = pl.BlockSpec(memory_space=pl.ANY)
    vmem = pl.BlockSpec(memory_space=pltpu.VMEM)
    i32 = jnp.int32
    scratch = [
        pltpu.VMEM((half, nodes), i32),
        pltpu.VMEM((half, half), i32),
        pltpu.VMEM((cfg["h_rows"], halo), i32),
        pltpu.VMEM((fin, nodes), BF),
        pltpu.VMEM((FEAT_PAD, nodes), F32),
        pltpu.VMEM((half, nodes), BF),
        pltpu.VMEM((half, half), BF),
        pltpu.VMEM((halo, nodes), BF),
        pltpu.VMEM((halo, nodes), BF),
        pltpu.VMEM((2 * FEAT_PAD, nodes), BF),
        pltpu.VMEM((2, HID, nodes), BF),
        pltpu.VMEM((2, HID, nodes), BF),
        pltpu.VMEM((3, HID, half), BF),
        pltpu.VMEM((LANES, half), F32),
        pltpu.VMEM((HID, half), F32),
        pltpu.VMEM((2, HID, half), F32),
        pltpu.VMEM((2, 8, half), F32),
        pltpu.VMEM((8, half), F32),
        pltpu.VMEM((5, n_dom, 16, LANES), BF),
        pltpu.VMEM((5, n_dom, 16, LANES), BF),
        pltpu.VMEM((2 * win, LANES), F32),
        pltpu.VMEM((par_rows, HID), BF),
        pltpu.VMEM((2, n_dom * par_rows, HID), BF),
        pltpu.VMEM((2, ROWS_PAD, HID), BF),
        pltpu.VMEM((2, HID, ROWS_PAD), BF),
        pltpu.VMEM((HID, 8), F32),
        pltpu.VMEM((HID, LANES), BF),
        pltpu.VMEM((HID, LANES), BF),
        pltpu.VMEM((CLS_PAD, HID), BF),
        pltpu.VMEM((CLS_PAD, HID), BF),
        pltpu.VMEM((3, HID, half), BF),
        pltpu.VMEM((grad_rows, HID), F32),
        pltpu.VMEM((grad_rows, HID), F32),
        pltpu.VMEM((2, grad_rows, HID), F32),
        pltpu.VMEM((grad_rows, HID), F32),
        pltpu.VMEM((n_dom, win, HID), F32),
        pltpu.VMEM((n_dom, win, HID), F32),
        pltpu.VMEM((HID, HID), F32),
        pltpu.VMEM((HID, LANES), F32),
        pltpu.VMEM((HID, LANES), F32),
        pltpu.VMEM((8, LANES), F32),
        pltpu.SemaphoreType.DMA((3 + half // 128,)),
        pltpu.SemaphoreType.DMA((7,)),
        pltpu.SemaphoreType.DMA((7,)),
        pltpu.SemaphoreType.DMA((5,)),
        pltpu.SemaphoreType.DMA((5,)),
        pltpu.SemaphoreType.DMA,
        pltpu.SemaphoreType.DMA,
        pltpu.SemaphoreType.DMA,
        pltpu.SemaphoreType.DMA,
    ]
    grad, scalars = pl.pallas_call(
        functools.partial(kernel, cfg),
        out_shape=(
            jax.ShapeDtypeStruct((2 * win, LANES), F32),
            jax.ShapeDtypeStruct((2, LANES), F32),
        ),
        in_specs=[hbm, hbm, hbm, vmem, vmem, vmem, vmem],
        out_specs=(vmem, vmem),
        scratch_shapes=scratch,
        compiler_params=pltpu.CompilerParams(
            collective_id=0, has_side_effects=True, vmem_limit_bytes=60 * 2**20
        ),
    )(
        features.T,
        local_mask,
        halo_mask,
        send_rows[0].T,
        labels.reshape(1, nodes),
        label_mask.reshape(1, nodes),
        master,
    )
    own_grad = grad.reshape(1, -1)[:, :shard]
    new_first = DECAY_ONE * first + (1.0 - DECAY_ONE) * own_grad
    new_second = DECAY_TWO * second + (1.0 - DECAY_TWO) * own_grad * own_grad
    first_hat = new_first / (1.0 - DECAY_ONE**STEP)
    second_hat = new_second / (1.0 - DECAY_TWO**STEP)
    new_master = master - LEARN_RATE * (
        first_hat / (jnp.sqrt(second_hat) + ADAM_EPS) + WEIGHT_DECAY * master
    )
    return (scalars[0, 0], scalars[1, 0], new_master, new_first, new_second)


def solution(mesh):
    in_specs = (
        P("dom", "feat"),
        P("dom", None),
        P("dom", None),
        P("dom", None, None),
        P("dom"),
        P("dom"),
        P("feat", "dom"),
        P("feat", "dom"),
        P("feat", "dom"),
    )
    out_specs = (P(), P(), P("feat", "dom"), P("feat", "dom"), P("feat", "dom"))
    return jax.shard_map(
        functools.partial(per_device, mesh.shape["dom"]),
        mesh=mesh, in_specs=in_specs, out_specs=out_specs, check_vma=False,
    )
```

time: 490 us -> 75.1 us (0.15)
  the two profiles are of different devices: /device:TPU:0 before, /device:TPU:13 now
where the time goes in v1:
time: 75.1 us; the launch traced here: 74.8 us
  Pallas kernels  71.3 us (95%)
  other arithmetic  1.55 us (2%)
  local copies, waits for them, and re-layouts  1.27 us (2%)
    pallas_call x1, Pallas kernels, per_device(): pl.pallas_call(functools.partial(kernel, cfg), out_shape=(jax.ShapeDtypeS...  71.3 us
    sub x1, other arithmetic, per_device(): master - LEARN_RATE * (first_hat / (jnp.sqrt(second_hat) + ADAM_EPS) + WE...  1.55 us

profile of v1, /device:TPU:13, one launch (start us, length us, event | category | flops | bytes accessed | tf_op | source)
XLA Modules:
  0.0 74.8 jit_solution(2776180146030167065)
XLA Ops:
  0.6 0.0 copy-start
  0.6 0.0 copy-start.2
  0.7 0.0 copy-start.1
  0.7 71.3 %shard_map.128 = (f32[64,128]{1,0:T(8,128)}, f32[2,128]{1,0:T(2,128)}) custom-call(bf16[50,2048]{1,0:T(8,128)(2,1)} %bitcast.9, s32[2048,2048]{1,0:T(8,128)} %lm_in.1, s32[2048,128]{1,0:T(8,128)} %hm_in.1, s32[8,16]{1,0:T(8,128)} %bitcast.13, s32[1,2048]{1,0:T(1,128)} %bitcast.11, s32[1,2048]{1,0:T(1,128)} %bitcast.12, f32[1,6480]{1,0:T(1,128)} %master_in.1), custom_call_target="tpu_custom_call" | custom-call | tf_op jit(solution)/shard_map/pallas_call | solution.py:616
  72.0 1.3 %fusion.2 = (f32[1,1]{1,0:T(1,128)}, f32[1,1]{1,0:T(1,128)}) fusion(f32[2,128]{1,0:T(2,128)} %get-tuple-element.7), kind=kLoop, calls=%fused_computation.4 | loop fusion | bytes 16 | tf_op jit(solution)/shard_map/slice | solution.py:645
  73.2 0.0 copy-done
  73.2 0.0 copy-done.2
  73.2 0.0 copy-done.1
  73.2 1.6 %multiply_subtract_fusion = (f32[1,6480]{1,0:T(1,128)}, f32[1,6480]{1,0:T(1,128)}, f32[1,6480]{1,0:T(1,128)}) fusion(f32[1,6480]{1,0:T(1,128)S(1)} %copy-done, f32[1,8192]{1,0:T(1,128)} %bitcast.10, f32[1,6480]{1,0:T(1,128)S(1)} %copy-done.1, f32[1,6480]{1,0:T(1,128)S(1)} %copy-done.2), kind=kLoop, calls=%fused_computation.2 | loop fusion | flops 97200 | bytes 181440 | tf_op jit(solution)/shard_map/sub | solution.py:642
Async XLA Ops:
  0.6 72.6 %copy-start = (f32[1,6480]{1,0:T(1,128)S(1)}, f32[1,6480]{1,0:T(1,128)}, u32[]{:S(2)}) copy-start(f32[1,6480]{1,0:T(1,128)} %master_in.1) | copy-start | bytes 77764
  0.6 72.6 %copy-start.2 = (f32[1,6480]{1,0:T(1,128)S(1)}, f32[1,6480]{1,0:T(1,128)}, u32[]{:S(2)}) copy-start(f32[1,6480]{1,0:T(1,128)} %param.17) | copy-start | bytes 77764
  0.7 72.6 %copy-start.1 = (f32[1,6480]{1,0:T(1,128)S(1)}, f32[1,6480]{1,0:T(1,128)}, u32[]{:S(2)}) copy-start(f32[1,6480]{1,0:T(1,128)} %param.16) | copy-start | bytes 77764

commit v2 on v1

v2 whole, which is shorter than its diff:
```python
import functools

import jax
import jax.numpy as jnp
from jax import lax
from jax.experimental import pallas as pl
from jax.experimental.pallas import tpu as pltpu
from jax.sharding import PartitionSpec as P

HID = 256
CLS = 47
STEP = 10
EPSILON = 1e-05
LEARN_RATE = 0.02
DECAY_ONE = 0.9
DECAY_TWO = 0.999
ADAM_EPS = 1e-08
WEIGHT_DECAY = 0.01

MESH = pl.DeviceIdType.MESH
BF = jnp.bfloat16
F32 = jnp.float32
LANES = 128
CLS_PAD = 64
FEAT_PAD = 64
HALF_HID = HID // 2
ROW_ONE = 2 * FEAT_PAD
ROW_TWO = ROW_ONE + 2 * HALF_HID
HEAD_ROWS = 2 * HALF_HID * CLS // HID
ROW_NORM = ROW_TWO + 48
GELU_A = 0.7978845608028654
GELU_B = 0.044715


def dot(a, b, ca=1, cb=0, precision=None):
    return lax.dot_general(
        a, b, (((ca,), (cb,)), ((), ())), precision=precision, preferred_element_type=F32
    )


def iota(shape, axis):
    return lax.broadcasted_iota(jnp.int32, shape, axis)


def gelu(x):
    half = 0.5 * x
    return half + half * jnp.tanh(x * (GELU_A + (GELU_A * GELU_B) * (x * x)))


def gelu_grad(x):
    xx = x * x
    t = jnp.tanh(x * (GELU_A + (GELU_A * GELU_B) * xx))
    return 0.5 + 0.5 * t + (x * (GELU_A + (3.0 * GELU_A * GELU_B) * xx)) * (0.5 - 0.5 * (t * t))


def roll_rows(x, amount, right):
    for bit in range(8):
        step = 1 << bit
        moved = pltpu.roll(x, step if right else HID - step, 1)
        x = jnp.where((amount & step) != 0, moved, x)
    return x


def loop(n, body):
    def step(i, carry):
        body(i)
        return carry

    lax.fori_loop(0, n, step, 0)


def kernel(
    cfg,
    x_in, lm_in, hm_in, send_hbm, label_hbm, lmask_hbm, master_hbm,
    grad_out, scalar_out,
    send_in, label_in, lmask_in, master_in,
    a_stage, b_stage, h_stage, x_stage,
    a_rows, b_far, hmt, sel, xs, hs, gs_all, agg_ref, agg_zero,
    edge_rows, edge_far, edge_hm, edge_x, edge_h, edge_mixed, edge_inv, part_tx, part_rx,
    mixed, normed, slope, scale_inv, inv_ref, halo_tx, halo_rx,
    flat_t, par_tx, par_rx, wmat, wmat_t, norm_col, head_ws, head_wn, head_ws_t, head_wn_t,
    g_low, grads, early_rx, late_rx, one_tx, one_rx, two_tx, two_rx, top_tx, top_one, top_two, dw_head, acc_gain, acc_bias, place,
    local_sem, pair_send, pair_recv, halo_send, halo_recv, par_send, column_recv, plane_recv,
    one_send, one_recv, two_send, two_recv, top_send, top_recv,
):
    n_dom, nodes, half, halo, shard, fin = (
        cfg["n_dom"], cfg["nodes"], cfg["half"], cfg["halo"], cfg["shard"], cfg["fin"]
    )
    win, par_rows, rows_all = cfg["win"], cfg["par_rows"], cfg["rows_all"]
    me, f = lax.axis_index("dom"), lax.axis_index("feat")
    other = 1 - f
    own = pl.multiple_of(f * half, half)
    far = pl.multiple_of(other * half, half)
    own_cols, far_cols = pl.ds(own, half), pl.ds(far, half)

    barrier = pltpu.get_barrier_semaphore()

    def greet(i):
        p = lax.rem(me + i + 1, n_dom)
        pl.semaphore_signal(barrier, inc=1, device_id=(p, f), device_id_type=MESH)

    loop(n_dom - 1, greet)
    pl.semaphore_signal(barrier, inc=1, device_id=(me, other), device_id_type=MESH)

    chunk = 128
    n_chunk = half // chunk
    x_copy = pltpu.make_async_copy(x_in, x_stage, local_sem.at[4])
    x_copy.start()
    small_copies = [
        pltpu.make_async_copy(src, dst, local_sem.at[k])
        for k, (src, dst) in enumerate(
            ((master_hbm, master_in), (send_hbm, send_in), (label_hbm, label_in),
             (lmask_hbm, lmask_in))
        )
    ]
    for copy in small_copies:
        copy.start()
    h_rows = cfg["h_rows"]

    def h_copy(i):
        return pltpu.make_async_copy(
            hm_in.at[pl.ds(i * h_rows, h_rows), :], h_stage, local_sem.at[5]
        )

    h_copy(0).start()

    slots = cfg["slots"]

    def a_copy(i):
        return pltpu.make_async_copy(
            lm_in.at[pl.ds(pl.multiple_of(own + i * chunk, chunk), chunk), :],
            a_stage.at[lax.rem(i, slots)], local_sem.at[6 + lax.rem(i, slots)],
        )

    def b_copy(i):
        return pltpu.make_async_copy(
            lm_in.at[pl.ds(pl.multiple_of(far + i * chunk, chunk), chunk), own_cols],
            b_stage.at[lax.rem(i, slots)], local_sem.at[6 + slots + lax.rem(i, slots)],
        )

    loop(slots, lambda i: a_copy(i).start())
    loop(slots, lambda i: b_copy(i).start())

    def pair_copy(src, dst, k):
        return pltpu.make_async_remote_copy(
            src_ref=src, dst_ref=dst, send_sem=pair_send.at[k], recv_sem=pair_recv.at[k],
            device_id=(me, other), device_id_type=MESH,
        )

    x_copy.wait()
    slice_rows = pl.ds(pl.multiple_of(f * FEAT_PAD, FEAT_PAD), FEAT_PAD)
    pad_rows = iota((FEAT_PAD, half), 0)
    for c in range(2):
        part = slice(c * half, (c + 1) * half)
        mixed[0:FEAT_PAD, :] = jnp.where(pad_rows == fin, 1.0, 0.0)
        mixed[0:fin, :] = x_stage[:, part].astype(F32)
        xs[slice_rows, part] = mixed[0:FEAT_PAD, :].astype(BF)

    pl.semaphore_wait(barrier, n_dom)

    x_pair = pair_copy(xs.at[slice_rows, :], xs.at[slice_rows, :], 0)
    x_pair.start()
    off = lax.rem(shard * me, HID)
    off_row, off_lane = off // LANES, lax.rem(off, LANES)
    t_rows = 2 * win
    lane_t = iota((t_rows, LANES), 1)

    def to_window(t):
        r = pltpu.roll(t, off_lane, 1)
        t = jnp.where(lane_t < off_lane, pltpu.roll(r, 1, 0), r)
        t = jnp.where(off_row == 1, pltpu.roll(t, 1, 0), t)
        flat_t[...] = t
        return jnp.concatenate(
            [flat_t[pl.ds(0, win, stride=2), :], flat_t[pl.ds(1, win, stride=2), :]], axis=1
        )

    def from_window(w):
        flat_t[pl.ds(0, win, stride=2), :] = w[:, :LANES]
        flat_t[pl.ds(1, win, stride=2), :] = w[:, LANES:]
        t = flat_t[...]
        t = jnp.where(off_row == 1, pltpu.roll(t, t_rows - 1, 0), t)
        back = lax.rem(LANES - off_lane, LANES)
        near = pltpu.roll(t, back, 1)
        after = pltpu.roll(near, t_rows - 1, 0)
        return jnp.where(lane_t + off_lane < LANES, near, after)

    small_copies[0].wait()
    flat_t[...] = jnp.zeros_like(flat_t)
    for k in range(-(-shard // LANES)):
        width = min(LANES, shard - k * LANES)
        flat_t[k : k + 1, 0:width] = master_in[0:1, k * LANES : k * LANES + width]
    window = to_window(flat_t[...])
    if par_rows > win:
        window = jnp.concatenate([window, jnp.zeros((par_rows - win, HID), F32)], axis=0)
    par_tx[...] = window.astype(BF)
    par_rx[f, pl.ds(pl.multiple_of(me * par_rows, par_rows), par_rows), :] = par_tx[...]


    group = cfg["group"]
    n_high = n_dom // group
    high, low = me // group, lax.rem(me, group)
    urgent = cfg["urgent"]
    patient = [h for h in range(n_high) if h not in urgent]

    def par_slot(h, w):
        start = pl.multiple_of((h * group + w) * par_rows, par_rows)
        return par_rx.at[f, pl.ds(start, par_rows), :]

    def par_send_to(h, w, src, slot_high, sem):
        pltpu.make_async_remote_copy(
            src_ref=src, dst_ref=par_slot(slot_high, low), send_sem=par_send, recv_sem=sem,
            device_id=(h * group + w, f), device_id_type=MESH,
        ).start()

    def par_plane(slot_high, src):
        for step in range(1, group):
            par_send_to(high, lax.rem(low + step, group), src, slot_high, plane_recv.at[slot_high])

    def send_params(which):
        is_one = functools.reduce(jnp.logical_or, [high == h for h in which])

        @pl.when(is_one)
        def _():
            for step in range(1, n_high):
                par_send_to(lax.rem(high + step, n_high), low, par_tx, high, column_recv.at[high])
            par_plane(high, par_tx)

    def forward_params(which):
        for h in which:
            @pl.when(high != h)
            def _():
                pltpu.make_async_copy(par_tx, par_tx, column_recv.at[h]).wait()
                par_plane(h, par_slot(h, low))

    def wait_params(which):
        part = pl.ds(0, (group - 1) * par_rows)
        for h in which:
            pltpu.make_async_copy(
                par_rx.at[f, part, :], par_rx.at[f, part, :], plane_recv.at[h]
            ).wait()

    def par_pairs(which, k):
        runs = []
        for h in which:
            if runs and runs[-1][1] == h:
                runs[-1][1] = h + 1
            else:
                runs.append([h, h + 1])
        copies = []
        for i, (start, end) in enumerate(runs):
            part = pl.ds(start * group * par_rows, (end - start) * group * par_rows)
            copies.append(pair_copy(par_rx.at[f, part, :], par_rx.at[f, part, :], k + i))
        return copies

    first_early = cfg["first_early"]
    send_params(urgent)
    small_copies[1].wait()
    send_rows = send_in[...].astype(F32)
    lane_d = iota(send_rows.shape, 1)
    node_lane = iota((16, nodes), 1).astype(F32)

    def build_sel(q):
        first = jnp.sum(jnp.where(lane_d == 2 * q, send_rows, 0.0), axis=1, keepdims=True)
        second = jnp.sum(jnp.where(lane_d == 2 * q + 1, send_rows, 0.0), axis=1, keepdims=True)
        rows = jnp.concatenate([first, second], axis=0)
        sel[pl.ds(pl.multiple_of(q * 16, 16), 16), :] = jnp.where(
            node_lane == rows, 1.0, 0.0
        ).astype(BF)

    if n_dom <= 16:
        for q in range(n_dom // 2):
            build_sel(q)
    else:
        loop(n_dom // 2, build_sel)

    def halo_copy(k, p):
        return pltpu.make_async_remote_copy(
            src_ref=halo_tx.at[k % 2, p], dst_ref=halo_rx.at[k, me],
            send_sem=halo_send.at[k], recv_sem=halo_recv.at[k],
            device_id=(p, f), device_id_type=MESH,
        )

    def send_halo(k):
        loop(n_dom - 1, lambda i: halo_copy(k, lax.rem(me + i + 1, n_dom)).start())
        halo_rx[k, me] = halo_tx[k % 2, me]

    def pack_halo(k, rows):
        v = rows.reshape(n_dom, 8, HID)
        if k >= 2:
            wait_halo_sent(k - 2)
        halo_tx[k % 2] = jnp.concatenate([v[:, :, :LANES], v[:, :, LANES:]], axis=1).astype(BF)

    def wait_halo(k):
        part = pl.ds(0, n_dom - 1)
        pltpu.make_async_copy(halo_rx.at[k, part], halo_rx.at[k, part], halo_recv.at[k]).wait()

    def wait_halo_sent(k):
        part = pl.ds(0, n_dom - 1)
        pltpu.make_async_copy(
            halo_tx.at[k % 2, part], halo_tx.at[k % 2, part], halo_send.at[k]
        ).wait()

    def read_halo(k):
        v = halo_rx[k].astype(F32)
        rows = jnp.concatenate(
            [v[:, :8, :].reshape(halo, LANES), v[:, 8:, :].reshape(halo, LANES)], axis=1
        )
        return rows.T.astype(BF)

    x_pair.wait_recv()
    picked = dot(sel[...], xs[...], 1, 1)
    edge_x[...] = picked.T.astype(BF)
    picked = picked.reshape(n_dom, 8, LANES)
    small_copies[2].wait()
    small_copies[3].wait()
    count = jnp.sum(lmask_in[...].astype(F32), axis=1, keepdims=True)
    count_high = jnp.floor(count * (1.0 / 256.0))
    count_low = count - 256.0 * count_high
    count_row = iota((8, LANES), 0)
    counts = jnp.where(count_row == 0, count_high, jnp.where(count_row == 1, count_low, 0.0))
    counts = jnp.broadcast_to(counts[None], (n_dom, 8, LANES))
    halo_tx[0] = jnp.concatenate([picked, counts], axis=1).astype(BF)
    send_halo(0)

    for i in range(nodes // h_rows):
        h_copy(i).wait()
        hmt[:, i * h_rows : (i + 1) * h_rows] = h_stage[...].astype(F32).T.astype(BF)
        if (i + 1) * h_rows < nodes:
            h_copy(i + 1).start()

    def convert_a(i):
        a_copy(i).wait()
        rows = pl.ds(pl.multiple_of(i * chunk, chunk), chunk)
        a_rows[rows, :] = a_stage[lax.rem(i, slots)].astype(F32).astype(BF)

        @pl.when(i + slots < n_chunk)
        def _():
            a_copy(i + slots).start()

    loop(n_chunk, convert_a)
    edge_hm[...] = dot(hmt[...], sel[...], 1, 1).astype(BF)

    def edge_chunk(q):
        rows = pl.ds(pl.multiple_of(q * LANES, LANES), LANES)
        edge_rows[rows, :] = dot(sel[rows, own_cols], a_rows[...]).astype(BF)

    loop(halo // LANES, edge_chunk)
    edge_pair = pair_copy(edge_rows, edge_far, 7)
    edge_pair.start()
    forward_params(urgent)
    send_params(patient)

    def build_place(q):
        rows = pl.ds(pl.multiple_of(q * 16, 16), 16)
        r_pad = iota((16, k_all), 0) + q * 16
        k_col = iota((16, k_all), 1)
        owner, inner = k_col // par_rows, lax.rem(k_col, par_rows)
        target = lax.shift_right_logical(owner * shard, 8) + inner
        row_of = jnp.where(
            r_pad < fin, r_pad,
            jnp.where(
                (r_pad >= FEAT_PAD) & (r_pad < FEAT_PAD + fin), r_pad - (FEAT_PAD - fin),
                jnp.where(
                    (r_pad >= ROW_ONE) & (r_pad < ROW_TWO + HEAD_ROWS),
                    r_pad - (ROW_ONE - 2 * fin), -1,
                ),
            ),
        )
        place[rows, :] = jnp.where(row_of == target, 1.0, 0.0).astype(BF)

    k_all = n_dom * par_rows
    loop(ROW_NORM // 16, build_place)
    mixed[0:LANES, :] = dot(xs[...], a_rows[...], 1, 1)
    def convert_b(i):
        b_copy(i).wait()
        rows = pl.ds(pl.multiple_of(i * chunk, chunk), chunk)
        b_far[rows, :] = b_stage[lax.rem(i, slots)].astype(F32).astype(BF)

        @pl.when(i + slots < n_chunk)
        def _():
            b_copy(i + slots).start()

    loop(n_chunk, convert_b)

    wait_params(urgent)
    par_urgent = par_pairs(urgent, 16)
    for copy in par_urgent:
        copy.start()
    wait_halo(0)
    arrived = halo_rx[0].astype(F32)
    halo_zero = arrived[:, :8, :].reshape(halo, LANES).T.astype(BF)
    count_all = jnp.sum(arrived[:, 8:, :], axis=0)
    label_count = 256.0 * count_all[0:1, 0:1] + count_all[1:2, 0:1]
    summed = mixed[0:LANES, :] + dot(halo_zero, hmt[:, own_cols])
    inverse = 1.0 / jnp.maximum(summed[fin : fin + 1, :], 1.0)
    inv_ref[...] = jnp.broadcast_to(inverse, inv_ref.shape)
    agg_zero[...] = (summed * inverse).astype(BF)
    edge_pair.wait()

    def edge_sum(q):
        rows = pl.ds(pl.multiple_of(q * LANES, LANES), LANES)
        edge_rows[rows, :] = edge_rows[rows, :] + edge_far[rows, :]

    loop(halo // LANES, edge_sum)
    summed = dot(xs[...], edge_rows[...], 1, 1) + dot(halo_zero, edge_hm[...])
    inverse = 1.0 / jnp.maximum(summed[fin : fin + 1, :], 1.0)
    edge_inv[...] = jnp.broadcast_to(inverse, edge_inv.shape)
    edge_agg = (summed * inverse).astype(BF)

    forward_params(patient)
    for copy in par_urgent:
        copy.wait_recv()
    k_first = first_early * par_rows
    norm_row = (n_dom - 1) * par_rows + rows_all - 2 - shard * (n_dom - 1) // HID
    w_zero = []
    for c in range(2):
        rows_t = dot(place[:ROW_ONE, :k_first], par_rx[c, :k_first, :]).T
        w_zero.append(rows_t.astype(BF))
        block = norm_row // 16 * 16
        norms = par_rx[c, block : block + 32, :].astype(F32) if block + 32 <= k_all else (
            par_rx[c, k_all - 32 : k_all, :].astype(F32)
        )
        block = min(block, k_all - 32)
        norms_t = jnp.concatenate([norms, jnp.zeros((LANES - 32, HID), F32)], axis=0).T
        for k in range(2):
            lane = norm_row - block + k
            col = norms_t[:, lane : lane + 1]
            norm_col[c * HALF_HID : (c + 1) * HALF_HID, 2 * k : 2 * k + 1] = col[:HALF_HID]
            norm_col[c * HALF_HID : (c + 1) * HALF_HID, 2 * k + 1 : 2 * k + 2] = col[HALF_HID:]
    w_zero = jnp.concatenate(w_zero, axis=1)

    def assemble_hidden():
        for c in range(2):
            rows = dot(place[ROW_ONE:ROW_TWO, :], par_rx[c])
            wmat[c] = rows.astype(BF)
            wmat_t[c] = rows.T.astype(BF)

    node = iota((HID, 48), 0)
    first_row = lax.shift_right_logical(node * CLS, 8)
    row_id = iota((HID, 48), 1)
    pick_a = jnp.where(row_id == first_row, 1.0, 0.0)
    pick_b = jnp.where(row_id == first_row + 1, 1.0, 0.0)
    start_lane = (iota((HID, HID), 0) * CLS) & (HID - 1)
    lane_w = iota((HID, HID), 1)

    def assemble_head():
        for c in range(2):
            flat = dot(place[ROW_TWO:ROW_NORM, :], par_rx[c]).astype(BF)
            lo, hi = dot(pick_a.astype(BF), flat), dot(pick_b.astype(BF), flat)
            wide = jnp.where(lane_w >= start_lane, lo, hi)
            wide = roll_rows(wide, start_lane, False)
            head = jnp.where(lane_w < CLS, wide, 0.0)[:, :LANES]
            head_t = head.T[:CLS_PAD]
            half_rows = slice(c * HALF_HID, (c + 1) * HALF_HID)
            head_ws[half_rows, :] = head[:HALF_HID].astype(BF)
            head_wn[half_rows, :] = head[HALF_HID:].astype(BF)
            head_ws_t[:, half_rows] = head_t[:, :HALF_HID].astype(BF)
            head_wn_t[:, half_rows] = head_t[:, HALF_HID:].astype(BF)

    wide_cols = 256
    n_cols = half // wide_cols

    def norm_apply(x, layer):
        centre = x - jnp.mean(x, axis=0, keepdims=True)
        rs = lax.rsqrt(jnp.mean(centre * centre, axis=0, keepdims=True) + EPSILON)
        n = centre * rs
        shifted = n * norm_col[:, 2 * layer : 2 * layer + 1] + norm_col[
            :, 2 * layer + 1 : 2 * layer + 2
        ]
        return n, rs, gelu(shifted).astype(BF)

    def norm_forward(layer, mix):
        for j in range(n_cols):
            cols = slice(j * wide_cols, (j + 1) * wide_cols)
            n, rs, value = norm_apply(mix(j * wide_cols), layer)
            normed[layer, :, cols] = n
            scale_inv[layer, :, cols] = jnp.broadcast_to(rs, (8, wide_cols))
            out = pl.ds(pl.multiple_of(own + j * wide_cols, wide_cols), wide_cols)
            hs[layer, :, out] = value

    def norm_slope(layer):
        def body(i):
            for j in range(2):
                cols = pl.ds(pl.multiple_of((2 * i + j) * LANES, LANES), LANES)
                shifted = normed[layer, :, cols] * norm_col[
                    :, 2 * layer : 2 * layer + 1
                ] + norm_col[:, 2 * layer + 1 : 2 * layer + 2]
                slope[layer, :, cols] = gelu_grad(shifted)

        loop(half // (2 * LANES), body)

    def norm_edge(layer):
        def body(j):
            cols = pl.ds(pl.multiple_of(j * LANES, LANES), LANES)
            edge_h[layer, :, cols] = norm_apply(edge_mixed[:, cols], layer)[2]

        loop(halo // LANES, body)
        pack_halo(1 + layer, edge_h[layer].astype(F32).T)
        send_halo(1 + layer)

    def rows_of(x, agg):
        return jnp.concatenate([x[:FEAT_PAD], agg[:FEAT_PAD], x[FEAT_PAD:], agg[FEAT_PAD:]], axis=0)

    x_own = xs[:, own_cols]
    agg_own = agg_zero[...]
    edge_mixed[...] = dot(w_zero, rows_of(edge_x[...], edge_agg))
    norm_edge(0)
    norm_forward(
        0, lambda c: dot(
            w_zero,
            rows_of(
                xs[:, pl.ds(pl.multiple_of(own + c, wide_cols), wide_cols)],
                agg_zero[:, c : c + wide_cols],
            ),
        ),
    )
    h_pair_one = pair_copy(hs.at[0, :, own_cols], hs.at[0, :, own_cols], 2)
    h_pair_one.start()
    mixed[...] = dot(hs[0, :, own_cols], a_rows[:, own_cols], 1, 1)
    wait_params(patient)
    par_rest = par_pairs(patient, 20)
    for copy in par_rest:
        copy.start()
    for copy in par_rest:
        copy.wait_recv()
    assemble_hidden()
    w_self_t = jnp.concatenate([wmat_t[0, :, :LANES], wmat_t[1, :, :LANES]], axis=1)
    w_neigh_t = jnp.concatenate([wmat_t[0, :, LANES:], wmat_t[1, :, LANES:]], axis=1)
    h_pair_one.wait_recv()
    mixed[...] += dot(hs[0, :, far_cols], a_rows[:, far_cols], 1, 1)
    edge_mixed[...] = dot(hs[0], edge_rows[...], 1, 1)
    wait_halo(1)
    halo_one = read_halo(1)
    edge_agg = ((edge_mixed[...] + dot(halo_one, edge_hm[...])) * edge_inv[0:1, :]).astype(BF)
    edge_mixed[...] = dot(w_self_t, edge_h[0]) + dot(w_neigh_t, edge_agg)
    norm_edge(1)
    agg_ref[0] = ((mixed[...] + dot(halo_one, hmt[:, own_cols])) * inv_ref[0:1, :]).astype(BF)
    norm_forward(
        1, lambda c: dot(w_self_t, hs[0, :, pl.ds(pl.multiple_of(own + c, wide_cols), wide_cols)])
        + dot(w_neigh_t, agg_ref[0, :, c : c + wide_cols]),
    )
    h_pair_two = pair_copy(hs.at[1, :, own_cols], hs.at[1, :, own_cols], 3)
    h_pair_two.start()
    mixed[...] = dot(hs[1, :, own_cols], a_rows[:, own_cols], 1, 1)
    assemble_head()
    h_pair_two.wait_recv()
    mixed[...] += dot(hs[1, :, far_cols], a_rows[:, far_cols], 1, 1)
    wait_halo(2)
    total = mixed[...] + dot(read_halo(2), hmt[:, own_cols])
    agg_ref[1] = (total * inv_ref[0:1, :]).astype(BF)

    logits = dot(head_ws_t[...], hs[1, :, own_cols]) + dot(head_wn_t[...], agg_ref[1])
    class_id = iota((CLS_PAD, half), 0)
    logits = jnp.where(class_id < CLS, logits, -1e30)
    top = jnp.max(logits, axis=0, keepdims=True)
    log_total = top + jnp.log(jnp.sum(jnp.exp(logits - top), axis=0, keepdims=True))
    onehot = class_id == label_in[0:1, own_cols]
    weight = lmask_in[0:1, own_cols].astype(F32)
    chosen = jnp.sum(jnp.where(onehot, logits, 0.0), axis=0, keepdims=True)
    loss_part = jnp.sum((log_total - chosen) * weight, axis=1, keepdims=True)
    pad_rows = grads.shape[1] - rows_all // 8 * 8
    for c in range(2):
        grads[c, rows_all // 8 * 8 :, :] = jnp.broadcast_to(loss_part, (pad_rows, HID))
    probs = jnp.exp(logits - log_total)
    g_logits = (probs - jnp.where(onehot, 1.0, 0.0)) * (weight / label_count)
    g_low[0:CLS_PAD, :] = g_logits.astype(BF)
    g_head = g_low[0:CLS_PAD, :]

    def exchange_backward(k):
        whole = pair_copy(gs_all.at[k, :, own_cols], gs_all.at[k, :, own_cols], 4 + k)
        part_tx[...] = dot(hmt[:, own_cols], gs_all[k, :, own_cols], 1, 1)
        part = pair_copy(part_tx, part_rx.at[k], 8 + k)
        part.start()
        whole.start()
        return whole, part

    def send_back(k, part):
        part.wait()
        pack_halo(3 + k, part_tx[...] + part_rx[k])
        send_halo(3 + k)

    def spread(k, whole, between=None):
        mixed[...] += dot(gs_all[k, :, own_cols], a_rows[:, own_cols])
        if between is not None:
            between()
        whole.wait_recv()
        mixed[...] += dot(gs_all[k, :, far_cols], b_far[...])
        if k == 1:
            norm_slope(0)
        wait_halo(3 + k)
        return read_halo(3 + k)

    def norm_backward(layer, back):
        acc_gain[...] = jnp.zeros_like(acc_gain)
        acc_bias[...] = jnp.zeros_like(acc_bias)

        gain = norm_col[:, 2 * layer : 2 * layer + 1]
        for j in range(n_cols):
            cols = slice(j * wide_cols, (j + 1) * wide_cols)
            n = normed[layer, :, cols]
            own_chunk = pl.ds(pl.multiple_of(own + j * wide_cols, wide_cols), wide_cols)
            g_shift = (mixed[:, cols] + dot(back, sel[:, own_chunk])) * slope[layer, :, cols]
            scaled = g_shift * n
            acc_gain[...] += scaled[:, :LANES] + scaled[:, LANES:]
            acc_bias[...] += g_shift[:, :LANES] + g_shift[:, LANES:]
            gn = g_shift * gain
            mean_one = jnp.mean(gn, axis=0, keepdims=True)
            mean_two = jnp.mean(gn * n, axis=0, keepdims=True)
            g_mixed = (gn - mean_one - n * mean_two) * scale_inv[layer, 0:1, cols]
            g_low[:, cols] = g_mixed.astype(BF)

        gain_row = jnp.sum(acc_gain[...].T, axis=0, keepdims=True)
        bias_row = jnp.sum(acc_bias[...].T, axis=0, keepdims=True)
        base = rows_all - 2 + layer
        for c in range(2):
            piece = slice(c * HALF_HID, (c + 1) * HALF_HID)
            grads[c, base : base + 1, :LANES] = gain_row[:, piece]
            grads[c, base : base + 1, LANES:] = bias_row[:, piece]

    early_start = shard * first_early // HID // 8 * 8
    early_rows = round_up(rows_all + 1, 8) - early_start

    norm_first = rows_all - 2
    top_start = rows_all // 8 * 8

    def stage_one(doms, far_ref):
        loss_row = grads[f, rows_all : rows_all + 1, :] + far_ref[rows_all : rows_all + 1, :]
        row = iota((win, HID), 0)
        for d in doms:
            start = shard * d // HID
            span = slice(start, start + win)
            rows = grads[f, span, :] + far_ref[span, :]
            if d == n_dom - 1:
                rows = jnp.where(row >= norm_first - start, 0.0, rows)
            rows = jnp.where(row == win - 1, loss_row, rows)
            to_high, to_low = d // group, d % group

            @pl.when(low == to_low)
            def _():
                one_rx[to_high, low] = rows

            @pl.when(low != to_low)
            def _():
                one_tx[d] = rows
                pltpu.make_async_remote_copy(
                    src_ref=one_tx.at[d], dst_ref=one_rx.at[to_high, low],
                    send_sem=one_send, recv_sem=one_recv.at[to_high],
                    device_id=(high * group + to_low, f), device_id_type=MESH,
                ).start()

    def top_copy(k, dst, p):
        return pltpu.make_async_remote_copy(
            src_ref=top_tx.at[k], dst_ref=dst, send_sem=top_send.at[k], recv_sem=top_recv.at[k],
            device_id=(p, f), device_id_type=MESH,
        )

    def stage_two(doms):
        for d in doms:
            to_high, to_low = d // group, d % group

            @pl.when(low == to_low)
            def _():
                part = pl.ds(0, group - 1)
                pltpu.make_async_copy(
                    one_rx.at[to_high, part], one_rx.at[to_high, part], one_recv.at[to_high]
                ).wait()
                total = jnp.sum(one_rx[to_high], axis=0)

                @pl.when(high == to_high)
                def _():
                    two_rx[high] = total

                @pl.when(high != to_high)
                def _():
                    two_tx[to_high] = total
                    pltpu.make_async_remote_copy(
                        src_ref=two_tx.at[to_high], dst_ref=two_rx.at[high],
                        send_sem=two_send, recv_sem=two_recv, device_id=(d, f),
                        device_id_type=MESH,
                    ).start()

    gs_all[0, :, own_cols] = (dot(head_wn[:, :CLS_PAD], g_head) * inv_ref[0:1, :]).astype(BF)
    g_pair_two, part_two = exchange_backward(0)
    mixed[...] = dot(head_ws[:, :CLS_PAD], g_head)
    dws = dot(hs[1, :, own_cols], g_head, 1, 1)
    dwn = dot(agg_ref[1], g_head, 1, 1)
    norm_slope(1)
    send_back(0, part_two)
    lane_h = iota((HID, HID), 1)
    for c in range(2):
        piece = slice(c * HALF_HID, (c + 1) * HALF_HID)
        dw_head[...] = jnp.zeros_like(dw_head)
        dw_head[:HALF_HID, :CLS_PAD] = dws[piece]
        dw_head[HALF_HID:, :CLS_PAD] = dwn[piece]
        wide = roll_rows(dw_head[...], start_lane, True)
        low_part = jnp.where(lane_h >= start_lane, wide, 0.0)
        high_part = jnp.where(lane_h >= start_lane, 0.0, wide)
        flat = dot(pick_a, low_part, 0, 0, lax.Precision.HIGHEST) + dot(
            pick_b, high_part, 0, 0, lax.Precision.HIGHEST
        )
        base = 2 * fin + 2 * HALF_HID
        grads[c, base : base + HEAD_ROWS, :] = flat[:HEAD_ROWS]
    back = spread(0, g_pair_two)
    norm_backward(1, back)

    g_one = g_low[...]
    w_self = jnp.concatenate(
        [wmat[0, :LANES], wmat[1, :LANES]], axis=0
    )
    w_neigh = jnp.concatenate(
        [wmat[0, LANES:], wmat[1, LANES:]], axis=0
    )
    gs_all[1, :, own_cols] = (dot(w_neigh, g_one) * inv_ref[0:1, :]).astype(BF)
    g_pair_one, part_one = exchange_backward(1)
    mixed[...] = dot(w_self, g_one)
    dws = dot(hs[0, :, own_cols], g_one, 1, 1)
    dwn = dot(agg_ref[0], g_one, 1, 1)
    for c in range(2):
        piece = slice(c * HALF_HID, (c + 1) * HALF_HID)
        base = 2 * fin
        grads[c, base : base + HALF_HID, :] = dws[piece]
        grads[c, base + HALF_HID : base + 2 * HALF_HID, :] = dwn[piece]

    def early_out():
        early_pair.wait()
        stage_one(range(first_early, n_dom), early_rx)

    early_pair = pair_copy(
        grads.at[other, pl.ds(early_start, early_rows), :],
        early_rx.at[pl.ds(early_start, early_rows), :], 6,
    )
    early_pair.start()
    send_back(1, part_one)
    back = spread(1, g_pair_one, early_out)
    norm_backward(0, back)

    g_zero = g_low[...]
    dws = dot(x_own, g_zero, 1, 1)
    dwn = dot(agg_own, g_zero, 1, 1)
    for c in range(2):
        start = c * FEAT_PAD
        grads[c, 0:fin, :] = dws[start : start + fin]
        grads[c, fin : 2 * fin, :] = dwn[start : start + fin]

    low_rows = pl.ds(0, round_up(shard * (first_early - 1) // HID + win, 8))
    top_rows = pl.ds(top_start, 8)
    late_pairs = [
        pair_copy(grads.at[other, rows, :], late_rx.at[rows, :], k)
        for rows, k in ((low_rows, 12), (top_rows, 13))
    ]
    for copy in late_pairs:
        copy.start()
    stage_two(range(first_early, n_dom))
    for copy in late_pairs:
        copy.wait_recv()
    stage_one(range(first_early), late_rx)
    norms = grads[f, top_rows, :] + late_rx[top_rows, :]
    top_tx[0] = norms

    @pl.when(low == group - 1)
    def _():
        top_one[low] = norms

    @pl.when(low != group - 1)
    def _():
        top_copy(0, top_one.at[low], high * group + group - 1).start()

    stage_two(range(first_early))

    @pl.when(low == group - 1)
    def _():
        part = pl.ds(0, group - 1)
        pltpu.make_async_copy(top_one.at[part], top_one.at[part], top_recv.at[0]).wait()
        norms = jnp.sum(top_one[...], axis=0)
        top_tx[1] = norms

        @pl.when(high == n_high - 1)
        def _():
            top_two[high] = norms

        @pl.when(high != n_high - 1)
        def _():
            top_copy(1, top_two.at[high], n_dom - 1).start()

    part = pl.ds(0, n_high - 1)
    pltpu.make_async_copy(two_rx.at[part], two_rx.at[part], two_recv).wait()

    @pl.when(me == n_dom - 1)
    def _():
        pltpu.make_async_copy(top_two.at[part], top_two.at[part], top_recv.at[1]).wait()
        norms = jnp.sum(top_two[...], axis=0)
        first = norm_first - shard * (n_dom - 1) // HID
        two_rx[0, first : first + 2, :] += norms[norm_first - top_start : norm_first - top_start + 2]

    total = jnp.sum(two_rx[...], axis=0)
    scalar_out[0:1, :] = total[win - 1 : win, :LANES]
    scalar_out[1:2, :] = jnp.broadcast_to(label_count, (1, LANES))
    total = jnp.where(iota((win, HID), 0) == win - 1, 0.0, total)
    flat_t[...] = from_window(total)
    for k in range(-(-shard // LANES)):
        width = min(LANES, shard - k * LANES)
        grad_out[0:1, k * LANES : k * LANES + width] = flat_t[k : k + 1, 0:width]

    for copy in (
        x_pair, h_pair_one, h_pair_two, g_pair_two, g_pair_one,
        *par_urgent, *par_rest, *late_pairs,
    ):
        copy.wait_send()
    for k in range(3, 5):
        wait_halo_sent(k)
    pltpu.make_async_copy(two_tx.at[part], two_tx.at[part], two_send).wait()
    @pl.when(low != group - 1)
    def _():
        pltpu.make_async_copy(top_tx.at[0], top_tx.at[0], top_send.at[0]).wait()

    @pl.when((low == group - 1) & (high != n_high - 1))
    def _():
        pltpu.make_async_copy(top_tx.at[1], top_tx.at[1], top_send.at[1]).wait()

    part = pl.ds(0, n_dom - n_high)
    pltpu.make_async_copy(one_tx.at[part], one_tx.at[part], one_send).wait()
    part = pl.ds(0, (n_dom - 1) * par_rows)
    pltpu.make_async_copy(par_rx.at[f, part, :], par_rx.at[f, part, :], par_send).wait()


def round_up(value, step):
    return -(-value // step) * step


def per_device(n_dom, features, local_mask, halo_mask, send_rows, labels, label_mask, master, first, second):
    nodes, halo = local_mask.shape[1], halo_mask.shape[1]
    half, shard, fin = nodes // 2, master.shape[1], features.shape[1]
    rows_all = n_dom * shard // HID
    span = (shard + HID - 2) // HID + 1
    win = round_up(span + 1, 8)
    par_rows = round_up(span, 16)
    grad_rows = round_up(rows_all + win, 8)
    group = 1
    while (2 * group) ** 2 <= n_dom:
        group *= 2
    head_end = 2 * fin + 2 * HALF_HID + HEAD_ROWS
    first_early = -(-2 * fin * HID // shard)
    assert shard * (n_dom - 1) <= (rows_all - 2) * HID and rows_all % 8 > 2
    urgent = sorted({d // group for d in range(first_early)} | {n_dom // group - 1})
    cfg = dict(
        group=group, first_early=first_early, urgent=urgent,
        n_dom=n_dom, nodes=nodes, half=half, halo=halo, shard=shard, fin=fin, win=win,
        par_rows=par_rows, rows_all=rows_all, grad_rows=grad_rows,
        h_rows=min(nodes, 2**18 // halo), slots=half // LANES if halo <= 256 else 2,
    )
    hbm = pl.BlockSpec(memory_space=pl.ANY)
    vmem = pl.BlockSpec(memory_space=pltpu.VMEM)
    i32 = jnp.int32
    scratch = [
        pltpu.VMEM((8, n_dom), i32),
        pltpu.VMEM((1, nodes), i32),
        pltpu.VMEM((1, nodes), i32),
        pltpu.VMEM((1, shard), F32),
        pltpu.VMEM((cfg["slots"], LANES, nodes), i32),
        pltpu.VMEM((cfg["slots"], LANES, half), i32),
        pltpu.VMEM((cfg["h_rows"], halo), i32),
        pltpu.VMEM((fin, nodes), BF),
        pltpu.VMEM((half, nodes), BF),
        pltpu.VMEM((half, half), BF),
        pltpu.VMEM((halo, nodes), BF),
        pltpu.VMEM((halo, nodes), BF),
        pltpu.VMEM((2 * FEAT_PAD, nodes), BF),
        pltpu.VMEM((2, HID, nodes), BF),
        pltpu.VMEM((2, HID, nodes), BF),
        pltpu.VMEM((2, HID, half), BF),
        pltpu.VMEM((LANES, half), BF),
        pltpu.VMEM((halo, nodes), BF),
        pltpu.VMEM((halo, nodes), BF),
        pltpu.VMEM((halo, halo), BF),
        pltpu.VMEM((LANES, halo), BF),
        pltpu.VMEM((2, HID, halo), BF),
        pltpu.VMEM((HID, halo), F32),
        pltpu.VMEM((8, halo), F32),
        pltpu.VMEM((halo, HID), F32),
        pltpu.VMEM((2, halo, HID), F32),
        pltpu.VMEM((HID, half), F32),
        pltpu.VMEM((2, HID, half), F32),
        pltpu.VMEM((2, HID, half), F32),
        pltpu.VMEM((2, 8, half), F32),
        pltpu.VMEM((8, half), F32),
        pltpu.VMEM((2, n_dom, 16, LANES), BF),
        pltpu.VMEM((5, n_dom, 16, LANES), BF),
        pltpu.VMEM((2 * win, LANES), F32),
        pltpu.VMEM((par_rows, HID), BF),
        pltpu.VMEM((2, n_dom * par_rows, HID), BF),
        pltpu.VMEM((2, HID, HID), BF),
        pltpu.VMEM((2, HID, HID), BF),
        pltpu.VMEM((HID, 8), F32),
        pltpu.VMEM((HID, LANES), BF),
        pltpu.VMEM((HID, LANES), BF),
        pltpu.VMEM((CLS_PAD, HID), BF),
        pltpu.VMEM((CLS_PAD, HID), BF),
        pltpu.VMEM((HID, half), BF),
        pltpu.VMEM((2, grad_rows, HID), F32),
        pltpu.VMEM((grad_rows, HID), F32),
        pltpu.VMEM((grad_rows, HID), F32),
        pltpu.VMEM((n_dom, win, HID), F32),
        pltpu.VMEM((n_dom // group, group, win, HID), F32),
        pltpu.VMEM((n_dom // group, win, HID), F32),
        pltpu.VMEM((n_dom // group, win, HID), F32),
        pltpu.VMEM((2, 8, HID), F32),
        pltpu.VMEM((group, 8, HID), F32),
        pltpu.VMEM((n_dom // group, 8, HID), F32),
        pltpu.VMEM((HID, HID), F32),
        pltpu.VMEM((HID, LANES), F32),
        pltpu.VMEM((HID, LANES), F32),
        pltpu.VMEM((ROW_NORM, n_dom * par_rows), BF),
        pltpu.SemaphoreType.DMA((6 + 2 * cfg["slots"],)),
        pltpu.SemaphoreType.DMA((24,)),
        pltpu.SemaphoreType.DMA((24,)),
        pltpu.SemaphoreType.DMA((5,)),
        pltpu.SemaphoreType.DMA((5,)),
        pltpu.SemaphoreType.DMA,
        pltpu.SemaphoreType.DMA((n_dom // group,)),
        pltpu.SemaphoreType.DMA((n_dom // group,)),
        pltpu.SemaphoreType.DMA,
        pltpu.SemaphoreType.DMA((n_dom // group,)),
        pltpu.SemaphoreType.DMA,
        pltpu.SemaphoreType.DMA,
        pltpu.SemaphoreType.DMA((2,)),
        pltpu.SemaphoreType.DMA((2,)),
    ]
    grad, scalars = pl.pallas_call(
        functools.partial(kernel, cfg),
        out_shape=(
            jax.ShapeDtypeStruct((1, shard), F32),
            jax.ShapeDtypeStruct((2, LANES), F32),
        ),
        in_specs=[hbm] * 7,
        out_specs=(vmem, vmem),
        scratch_shapes=scratch,
        compiler_params=pltpu.CompilerParams(
            collective_id=0, has_side_effects=True, vmem_limit_bytes=63 * 2**20
        ),
    )(
        features.T,
        local_mask,
        halo_mask,
        send_rows[0].T,
        labels.reshape(1, nodes),
        label_mask.reshape(1, nodes),
        master,
    )
    own_grad = grad
    new_first = DECAY_ONE * first + (1.0 - DECAY_ONE) * own_grad
    new_second = DECAY_TWO * second + (1.0 - DECAY_TWO) * own_grad * own_grad
    first_hat = new_first / (1.0 - DECAY_ONE**STEP)
    second_hat = new_second / (1.0 - DECAY_TWO**STEP)
    new_master = master - LEARN_RATE * (
        first_hat / (jnp.sqrt(second_hat) + ADAM_EPS) + WEIGHT_DECAY * master
    )
    return (scalars[0, 0], scalars[1, 0], new_master, new_first, new_second)


def solution(mesh):
    in_specs = (
        P("dom", "feat"),
        P("dom", None),
        P("dom", None),
        P("dom", None, None),
        P("dom"),
        P("dom"),
        P("feat", "dom"),
        P("feat", "dom"),
        P("feat", "dom"),
    )
    out_specs = (P(), P(), P("feat", "dom"), P("feat", "dom"), P("feat", "dom"))
    return jax.shard_map(
        functools.partial(per_device, mesh.shape["dom"]),
        mesh=mesh, in_specs=in_specs, out_specs=out_specs, check_vma=False,
    )
```

time: 75.1 us -> 57 us (0.76)
  the two profiles are of different devices: /device:TPU:13 before, /device:TPU:0 now
where the time goes in v2:
time: 57 us; the launch traced here: 56.8 us
  Pallas kernels  53.4 us (94%)
  other arithmetic  1.55 us (3%)
  local copies, waits for them, and re-layouts  1.27 us (2%)
  between operations  0.67 us (1%)
    pallas_call x1, Pallas kernels, per_device(): pl.pallas_call(functools.partial(kernel, cfg), out_shape=(jax.ShapeDtypeS...  53.4 us
    sub x1, other arithmetic, per_device(): master - LEARN_RATE * (first_hat / (jnp.sqrt(second_hat) + ADAM_EPS) + WE...  1.55 us
    slice x1, local copies, waits for them, and re-layouts, per_device(): return (scalars[0, 0], scalars[1, 0], new_master, new_first, new_second)  1.25 us

profile of v2, /device:TPU:0, one launch (start us, length us, event | category | flops | bytes accessed | tf_op | source)
XLA Modules:
  0.0 56.8 jit_solution(6865602570784591237)
XLA Ops:
  0.6 0.0 copy-start
  0.6 0.0 copy-start.2
  0.7 0.0 copy-start.1
  0.7 53.4 %shard_map.128 = (f32[1,6480]{1,0:T(1,128)}, f32[2,128]{1,0:T(2,128)}) custom-call(bf16[50,2048]{1,0:T(8,128)(2,1)} %bitcast.8, s32[2048,2048]{1,0:T(8,128)} %lm_in.1, s32[2048,128]{1,0:T(8,128)} %hm_in.1, s32[8,16]{1,0:T(8,128)} %bitcast.11, s32[1,2048]{1,0:T(1,128)} %bitcast.9, s32[1,2048]{1,0:T(1,128)} %bitcast.10, f32[1,6480]{1,0:T(1,128)} %master_hbm.1), custom_call_target="tpu_custom_call" | custom-call | tf_op jit(solution)/shard_map/pallas_call | solution.py:928
  54.0 1.3 %fusion.2 = (f32[1,1]{1,0:T(1,128)}, f32[1,1]{1,0:T(1,128)}) fusion(f32[2,128]{1,0:T(2,128)} %get-tuple-element.7), kind=kLoop, calls=%fused_computation.4 | loop fusion | bytes 16 | tf_op jit(solution)/shard_map/slice | solution.py:957
  55.3 0.0 copy-done
  55.3 0.0 copy-done.2
  55.3 0.0 copy-done.1
  55.3 1.6 %multiply_subtract_fusion = (f32[1,6480]{1,0:T(1,128)}, f32[1,6480]{1,0:T(1,128)}, f32[1,6480]{1,0:T(1,128)}) fusion(f32[1,6480]{1,0:T(1,128)S(1)} %copy-done, f32[1,6480]{1,0:T(1,128)} %get-tuple-element.8, f32[1,6480]{1,0:T(1,128)S(1)} %copy-done.1, f32[1,6480]{1,0:T(1,128)S(1)} %copy-done.2), kind=kLoop, calls=%fused_computation.2 | loop fusion | flops 97200 | bytes 181440 | tf_op jit(solution)/shard_map/sub | solution.py:954
Async XLA Ops:
  0.6 54.6 %copy-start = (f32[1,6480]{1,0:T(1,128)S(1)}, f32[1,6480]{1,0:T(1,128)}, u32[]{:S(2)}) copy-start(f32[1,6480]{1,0:T(1,128)} %master_hbm.1) | copy-start | bytes 77764
  0.6 54.6 %copy-start.2 = (f32[1,6480]{1,0:T(1,128)S(1)}, f32[1,6480]{1,0:T(1,128)}, u32[]{:S(2)}) copy-start(f32[1,6480]{1,0:T(1,128)} %param.17) | copy-start | bytes 77764
  0.7 54.6 %copy-start.1 = (f32[1,6480]{1,0:T(1,128)S(1)}, f32[1,6480]{1,0:T(1,128)}, u32[]{:S(2)}) copy-start(f32[1,6480]{1,0:T(1,128)} %param.16) | copy-start | bytes 77764

commit v3 on v2

--- a/solution.py
+++ b/solution.py
@@ -54,11 +54,18 @@
 
 
 def roll_rows(x, amount, right):
-    for bit in range(8):
+    for bit in range(7):
         step = 1 << bit
-        moved = pltpu.roll(x, step if right else HID - step, 1)
+        moved = pltpu.roll(x, step if right else LANES - step, 1)
         x = jnp.where((amount & step) != 0, moved, x)
     return x
+
+
+def parts(x):
+    first = x.astype(BF)
+    rest = x - first.astype(F32)
+    second = rest.astype(BF)
+    return first, second, (rest - second.astype(F32)).astype(BF)
 
 
 def loop(n, body):
@@ -76,11 +83,11 @@
     send_in, label_in, lmask_in, master_in,
     a_stage, b_stage, h_stage, x_stage,
     a_rows, b_far, hmt, sel, xs, hs, gs_all, agg_ref, agg_zero,
-    edge_rows, edge_far, edge_hm, edge_x, edge_h, edge_mixed, edge_inv, part_tx, part_rx,
+    edge_far, edge_hm, edge_x, edge_h, edge_inv, part_tx, part_rx,
     mixed, normed, slope, scale_inv, inv_ref, halo_tx, halo_rx,
-    flat_t, par_tx, par_rx, wmat, wmat_t, norm_col, head_ws, head_wn, head_ws_t, head_wn_t,
+    flat_t, par_tx, par_rx, norm_rx, wmat, wmat_t, norm_col, head_ws, head_wn, head_ws_t, head_wn_t,
     g_low, grads, early_rx, late_rx, one_tx, one_rx, two_tx, two_rx, top_tx, top_one, top_two, dw_head, acc_gain, acc_bias, place,
-    local_sem, pair_send, pair_recv, halo_send, halo_recv, par_send, column_recv, plane_recv,
+    local_sem, pair_send, pair_recv, halo_send, halo_recv, par_send, column_recv, plane_recv, norm_send, norm_recv,
     one_send, one_recv, two_send, two_recv, top_send, top_recv,
 ):
     n_dom, nodes, half, halo, shard, fin = (
@@ -93,14 +100,17 @@
     far = pl.multiple_of(other * half, half)
     own_cols, far_cols = pl.ds(own, half), pl.ds(far, half)
 
+    group = cfg["group"]
+    n_high = n_dom // group
+    high, low = me // group, lax.rem(me, group)
     barrier = pltpu.get_barrier_semaphore()
 
-    def greet(i):
-        p = lax.rem(me + i + 1, n_dom)
-        pl.semaphore_signal(barrier, inc=1, device_id=(p, f), device_id_type=MESH)
-
-    loop(n_dom - 1, greet)
-    pl.semaphore_signal(barrier, inc=1, device_id=(me, other), device_id_type=MESH)
+    def greet(p, core):
+        pl.semaphore_signal(barrier, inc=1, device_id=(p, core), device_id_type=MESH)
+
+    loop(n_dom - 1, lambda i: greet(lax.rem(me + i + 1, n_dom), f))
+    for step in range(group):
+        greet(high * group + lax.rem(low + step, group), other)
 
     chunk = 128
     n_chunk = half // chunk
@@ -152,108 +162,10 @@
     pad_rows = iota((FEAT_PAD, half), 0)
     for c in range(2):
         part = slice(c * half, (c + 1) * half)
-        mixed[0:FEAT_PAD, :] = jnp.where(pad_rows == fin, 1.0, 0.0)
-        mixed[0:fin, :] = x_stage[:, part].astype(F32)
-        xs[slice_rows, part] = mixed[0:FEAT_PAD, :].astype(BF)
-
-    pl.semaphore_wait(barrier, n_dom)
-
-    x_pair = pair_copy(xs.at[slice_rows, :], xs.at[slice_rows, :], 0)
-    x_pair.start()
-    off = lax.rem(shard * me, HID)
-    off_row, off_lane = off // LANES, lax.rem(off, LANES)
-    t_rows = 2 * win
-    lane_t = iota((t_rows, LANES), 1)
-
-    def to_window(t):
-        r = pltpu.roll(t, off_lane, 1)
-        t = jnp.where(lane_t < off_lane, pltpu.roll(r, 1, 0), r)
-        t = jnp.where(off_row == 1, pltpu.roll(t, 1, 0), t)
-        flat_t[...] = t
-        return jnp.concatenate(
-            [flat_t[pl.ds(0, win, stride=2), :], flat_t[pl.ds(1, win, stride=2), :]], axis=1
-        )
-
-    def from_window(w):
-        flat_t[pl.ds(0, win, stride=2), :] = w[:, :LANES]
-        flat_t[pl.ds(1, win, stride=2), :] = w[:, LANES:]
-        t = flat_t[...]
-        t = jnp.where(off_row == 1, pltpu.roll(t, t_rows - 1, 0), t)
-        back = lax.rem(LANES - off_lane, LANES)
-        near = pltpu.roll(t, back, 1)
-        after = pltpu.roll(near, t_rows - 1, 0)
-        return jnp.where(lane_t + off_lane < LANES, near, after)
-
-    small_copies[0].wait()
-    flat_t[...] = jnp.zeros_like(flat_t)
-    for k in range(-(-shard // LANES)):
-        width = min(LANES, shard - k * LANES)
-        flat_t[k : k + 1, 0:width] = master_in[0:1, k * LANES : k * LANES + width]
-    window = to_window(flat_t[...])
-    if par_rows > win:
-        window = jnp.concatenate([window, jnp.zeros((par_rows - win, HID), F32)], axis=0)
-    par_tx[...] = window.astype(BF)
-    par_rx[f, pl.ds(pl.multiple_of(me * par_rows, par_rows), par_rows), :] = par_tx[...]
-
-
-    group = cfg["group"]
-    n_high = n_dom // group
-    high, low = me // group, lax.rem(me, group)
-    urgent = cfg["urgent"]
-    patient = [h for h in range(n_high) if h not in urgent]
-
-    def par_slot(h, w):
-        start = pl.multiple_of((h * group + w) * par_rows, par_rows)
-        return par_rx.at[f, pl.ds(start, par_rows), :]
-
-    def par_send_to(h, w, src, slot_high, sem):
-        pltpu.make_async_remote_copy(
-            src_ref=src, dst_ref=par_slot(slot_high, low), send_sem=par_send, recv_sem=sem,
-            device_id=(h * group + w, f), device_id_type=MESH,
-        ).start()
-
-    def par_plane(slot_high, src):
-        for step in range(1, group):
-            par_send_to(high, lax.rem(low + step, group), src, slot_high, plane_recv.at[slot_high])
-
-    def send_params(which):
-        is_one = functools.reduce(jnp.logical_or, [high == h for h in which])
-
-        @pl.when(is_one)
-        def _():
-            for step in range(1, n_high):
-                par_send_to(lax.rem(high + step, n_high), low, par_tx, high, column_recv.at[high])
-            par_plane(high, par_tx)
-
-    def forward_params(which):
-        for h in which:
-            @pl.when(high != h)
-            def _():
-                pltpu.make_async_copy(par_tx, par_tx, column_recv.at[h]).wait()
-                par_plane(h, par_slot(h, low))
-
-    def wait_params(which):
-        part = pl.ds(0, (group - 1) * par_rows)
-        for h in which:
-            pltpu.make_async_copy(
-                par_rx.at[f, part, :], par_rx.at[f, part, :], plane_recv.at[h]
-            ).wait()
-
-    def par_pairs(which, k):
-        runs = []
-        for h in which:
-            if runs and runs[-1][1] == h:
-                runs[-1][1] = h + 1
-            else:
-                runs.append([h, h + 1])
-        copies = []
-        for i, (start, end) in enumerate(runs):
-            part = pl.ds(start * group * par_rows, (end - start) * group * par_rows)
-            copies.append(pair_copy(par_rx.at[f, part, :], par_rx.at[f, part, :], k + i))
-        return copies
-
-    first_early = cfg["first_early"]
-    send_params(urgent)
+        mixed[0:FEAT_PAD, :half] = jnp.where(pad_rows == fin, 1.0, 0.0)
+        mixed[0:fin, :half] = x_stage[:, part].astype(F32)
+        xs[slice_rows, part] = mixed[0:FEAT_PAD, :half].astype(BF)
+
     small_copies[1].wait()
     send_rows = send_in[...].astype(F32)
     lane_d = iota(send_rows.shape, 1)
@@ -306,49 +218,6 @@
             [v[:, :8, :].reshape(halo, LANES), v[:, 8:, :].reshape(halo, LANES)], axis=1
         )
         return rows.T.astype(BF)
-
-    x_pair.wait_recv()
-    picked = dot(sel[...], xs[...], 1, 1)
-    edge_x[...] = picked.T.astype(BF)
-    picked = picked.reshape(n_dom, 8, LANES)
-    small_copies[2].wait()
-    small_copies[3].wait()
-    count = jnp.sum(lmask_in[...].astype(F32), axis=1, keepdims=True)
-    count_high = jnp.floor(count * (1.0 / 256.0))
-    count_low = count - 256.0 * count_high
-    count_row = iota((8, LANES), 0)
-    counts = jnp.where(count_row == 0, count_high, jnp.where(count_row == 1, count_low, 0.0))
-    counts = jnp.broadcast_to(counts[None], (n_dom, 8, LANES))
-    halo_tx[0] = jnp.concatenate([picked, counts], axis=1).astype(BF)
-    send_halo(0)
-
-    for i in range(nodes // h_rows):
-        h_copy(i).wait()
-        hmt[:, i * h_rows : (i + 1) * h_rows] = h_stage[...].astype(F32).T.astype(BF)
-        if (i + 1) * h_rows < nodes:
-            h_copy(i + 1).start()
-
-    def convert_a(i):
-        a_copy(i).wait()
-        rows = pl.ds(pl.multiple_of(i * chunk, chunk), chunk)
-        a_rows[rows, :] = a_stage[lax.rem(i, slots)].astype(F32).astype(BF)
-
-        @pl.when(i + slots < n_chunk)
-        def _():
-            a_copy(i + slots).start()
-
-    loop(n_chunk, convert_a)
-    edge_hm[...] = dot(hmt[...], sel[...], 1, 1).astype(BF)
-
-    def edge_chunk(q):
-        rows = pl.ds(pl.multiple_of(q * LANES, LANES), LANES)
-        edge_rows[rows, :] = dot(sel[rows, own_cols], a_rows[...]).astype(BF)
-
-    loop(halo // LANES, edge_chunk)
-    edge_pair = pair_copy(edge_rows, edge_far, 7)
-    edge_pair.start()
-    forward_params(urgent)
-    send_params(patient)
 
     def build_place(q):
         rows = pl.ds(pl.multiple_of(q * 16, 16), 16)
@@ -370,7 +239,193 @@
 
     k_all = n_dom * par_rows
     loop(ROW_NORM // 16, build_place)
-    mixed[0:LANES, :] = dot(xs[...], a_rows[...], 1, 1)
+    for i in range(nodes // h_rows):
+        h_copy(i).wait()
+        hmt[:, i * h_rows : (i + 1) * h_rows] = h_stage[...].astype(F32).T.astype(BF)
+        if (i + 1) * h_rows < nodes:
+            h_copy(i + 1).start()
+
+    def convert_a(i):
+        a_copy(i).wait()
+        rows = pl.ds(pl.multiple_of(i * chunk, chunk), chunk)
+        a_rows[rows, :] = a_stage[lax.rem(i, slots)].astype(F32).astype(BF)
+
+        @pl.when(i + slots < n_chunk)
+        def _():
+            a_copy(i + slots).start()
+
+    pl.semaphore_wait(barrier, n_dom - 1 + group)
+
+    x_pair = pair_copy(xs.at[slice_rows, :], xs.at[slice_rows, :], 0)
+    x_pair.start()
+    off = lax.rem(shard * me, HID)
+    off_row, off_lane = off // LANES, lax.rem(off, LANES)
+    t_rows = 2 * win
+    lane_t = iota((t_rows, LANES), 1)
+
+    def to_window(t):
+        r = pltpu.roll(t, off_lane, 1)
+        t = jnp.where(lane_t < off_lane, pltpu.roll(r, 1, 0), r)
+        t = jnp.where(off_row == 1, pltpu.roll(t, 1, 0), t)
+        flat_t[...] = t
+        return jnp.concatenate(
+            [flat_t[pl.ds(0, win, stride=2), :], flat_t[pl.ds(1, win, stride=2), :]], axis=1
+        )
+
+    def from_window(w):
+        flat_t[pl.ds(0, win, stride=2), :] = w[:, :LANES]
+        flat_t[pl.ds(1, win, stride=2), :] = w[:, LANES:]
+        t = flat_t[...]
+        t = jnp.where(off_row == 1, pltpu.roll(t, t_rows - 1, 0), t)
+        back = lax.rem(LANES - off_lane, LANES)
+        near = pltpu.roll(t, back, 1)
+        after = pltpu.roll(near, t_rows - 1, 0)
+        return jnp.where(lane_t + off_lane < LANES, near, after)
+
+    small_copies[0].wait()
+    flat_t[...] = jnp.zeros_like(flat_t)
+    for k in range(-(-shard // LANES)):
+        width = min(LANES, shard - k * LANES)
+        flat_t[k : k + 1, 0:width] = master_in[0:1, k * LANES : k * LANES + width]
+    window = to_window(flat_t[...])
+    if par_rows > win:
+        window = jnp.concatenate([window, jnp.zeros((par_rows - win, HID), F32)], axis=0)
+    par_tx[...] = window.astype(BF)
+    par_rx[f, pl.ds(pl.multiple_of(me * par_rows, par_rows), par_rows), :] = par_tx[...]
+
+
+    urgent = cfg["urgent"]
+    patient = [h for h in range(n_high) if h not in urgent]
+
+    def par_slot(h, w):
+        start = pl.multiple_of((h * group + w) * par_rows, par_rows)
+        return par_rx.at[f, pl.ds(start, par_rows), :]
+
+    def send_to(p, core, src, dst, send_sem, recv_sem):
+        pltpu.make_async_remote_copy(
+            src_ref=src, dst_ref=dst, send_sem=send_sem, recv_sem=recv_sem,
+            device_id=(p, core), device_id_type=MESH,
+        ).start()
+
+    def to_plane(src, dst, send_sem, recv_sem, both):
+        if both:
+            send_to(me, other, src, dst, send_sem, recv_sem)
+        for step in range(1, group):
+            p = high * group + lax.rem(low + step, group)
+            send_to(p, f, src, dst, send_sem, recv_sem)
+            if both:
+                send_to(p, other, src, dst, send_sem, recv_sem)
+
+    def to_column(src, dst, send_sem, recv_sem):
+        for step in range(1, n_high):
+            p = lax.rem(high + step, n_high) * group + low
+            send_to(p, f, src, dst, send_sem, recv_sem)
+
+    def any_of(which):
+        return functools.reduce(jnp.logical_or, [high == h for h in which])
+
+    def own_params(which):
+        @pl.when(any_of(which))
+        def _():
+            to_plane(
+                par_tx, par_slot(high, low), par_send, plane_recv.at[high], which is urgent
+            )
+
+    def forward_params(which):
+        for h in which:
+            @pl.when(high != h)
+            def _():
+                pltpu.make_async_copy(par_tx, par_tx, column_recv.at[h]).wait()
+                to_plane(
+                    par_slot(h, low), par_slot(h, low), par_send, plane_recv.at[h],
+                    which is urgent,
+                )
+
+    def wait_params(which):
+        part = pl.ds(0, (2 * group - 1 if which is urgent else group - 1) * par_rows)
+        for h in which:
+            pltpu.make_async_copy(
+                par_rx.at[f, part, :], par_rx.at[f, part, :], plane_recv.at[h]
+            ).wait()
+
+    norm_local = rows_all - 2 - shard * (n_dom - 1) // HID
+    norm_block = norm_local // 16 * 16
+    norm_own = norm_rx.at[f]
+    last_low = low == group - 1
+
+    def send_norms():
+        @pl.when(me == n_dom - 1)
+        def _():
+            norm_rx[f] = par_tx[norm_block : norm_block + 16, :]
+            to_column(norm_own, norm_own, norm_send.at[0], norm_recv.at[0])
+
+    def forward_norms():
+        @pl.when(last_low)
+        def _():
+            @pl.when(high != n_high - 1)
+            def _():
+                pltpu.make_async_copy(norm_own, norm_own, norm_recv.at[0]).wait()
+
+            to_plane(norm_own, norm_own, norm_send.at[1], norm_recv.at[1], True)
+
+    def wait_norms():
+        @pl.when(last_low)
+        def _():
+            pltpu.make_async_copy(norm_own, norm_own, norm_recv.at[1]).wait()
+
+        @pl.when(jnp.logical_not(last_low))
+        def _():
+            pltpu.make_async_copy(norm_rx, norm_rx, norm_recv.at[1]).wait()
+
+    def par_pairs(which, k):
+        runs = []
+        for h in which:
+            if runs and runs[-1][1] == h:
+                runs[-1][1] = h + 1
+            else:
+                runs.append([h, h + 1])
+        copies = []
+        for i, (start, end) in enumerate(runs):
+            part = pl.ds(start * group * par_rows, (end - start) * group * par_rows)
+            copies.append(pair_copy(par_rx.at[f, part, :], par_rx.at[f, part, :], k + i))
+        return copies
+
+    first_early = cfg["first_early"]
+    to_column(par_tx, par_slot(high, low), par_send, column_recv.at[high])
+    own_params(urgent)
+    send_norms()
+    loop(n_chunk, convert_a)
+    edge_hm[...] = dot(hmt[...], sel[...], 1, 1).astype(BF)
+
+    def edge_chunk(q):
+        rows = pl.ds(pl.multiple_of(q * LANES, LANES), LANES)
+        a_rows[pl.ds(pl.multiple_of(half + q * LANES, LANES), LANES), :] = dot(
+            sel[rows, own_cols], a_rows[:half, :]
+        ).astype(BF)
+
+    loop(halo // LANES, edge_chunk)
+    edge_pair = pair_copy(a_rows.at[pl.ds(half, halo), :], edge_far, 7)
+    edge_pair.start()
+    x_pair.wait_recv()
+    picked = dot(sel[...], xs[...], 1, 1)
+    edge_x[...] = picked.T.astype(BF)
+    picked = picked.reshape(n_dom, 8, LANES)
+    small_copies[2].wait()
+    small_copies[3].wait()
+    count = jnp.sum(lmask_in[...].astype(F32), axis=1, keepdims=True)
+    count_high = jnp.floor(count * (1.0 / 256.0))
+    count_low = count - 256.0 * count_high
+    count_row = iota((8, LANES), 0)
+    counts = jnp.where(count_row == 0, count_high, jnp.where(count_row == 1, count_low, 0.0))
+    counts = jnp.broadcast_to(counts[None], (n_dom, 8, LANES))
+    halo_tx[0] = jnp.concatenate([picked, counts], axis=1).astype(BF)
+    send_halo(0)
+
+    forward_params(urgent)
+    forward_norms()
+    own_params(patient)
+    forward_params(patient)
+    mixed[0:LANES, :half] = dot(xs[...], a_rows[:half, :], 1, 1)
     def convert_b(i):
         b_copy(i).wait()
         rows = pl.ds(pl.multiple_of(i * chunk, chunk), chunk)
@@ -382,48 +437,32 @@
 
     loop(n_chunk, convert_b)
 
+    edge_pair.wait()
+
+    def edge_sum(q):
+        rows = pl.ds(pl.multiple_of(q * LANES, LANES), LANES)
+        ext = pl.ds(pl.multiple_of(half + q * LANES, LANES), LANES)
+        a_rows[ext, :] = a_rows[ext, :] + edge_far[rows, :]
+
+    loop(halo // LANES, edge_sum)
+    mixed[0:LANES, half : half + halo] = dot(xs[...], a_rows[half:, :], 1, 1)
     wait_params(urgent)
-    par_urgent = par_pairs(urgent, 16)
-    for copy in par_urgent:
-        copy.start()
+    wait_norms()
     wait_halo(0)
     arrived = halo_rx[0].astype(F32)
     halo_zero = arrived[:, :8, :].reshape(halo, LANES).T.astype(BF)
     count_all = jnp.sum(arrived[:, 8:, :], axis=0)
     label_count = 256.0 * count_all[0:1, 0:1] + count_all[1:2, 0:1]
-    summed = mixed[0:LANES, :] + dot(halo_zero, hmt[:, own_cols])
-    inverse = 1.0 / jnp.maximum(summed[fin : fin + 1, :], 1.0)
-    inv_ref[...] = jnp.broadcast_to(inverse, inv_ref.shape)
-    agg_zero[...] = (summed * inverse).astype(BF)
-    edge_pair.wait()
-
-    def edge_sum(q):
-        rows = pl.ds(pl.multiple_of(q * LANES, LANES), LANES)
-        edge_rows[rows, :] = edge_rows[rows, :] + edge_far[rows, :]
-
-    loop(halo // LANES, edge_sum)
-    summed = dot(xs[...], edge_rows[...], 1, 1) + dot(halo_zero, edge_hm[...])
-    inverse = 1.0 / jnp.maximum(summed[fin : fin + 1, :], 1.0)
-    edge_inv[...] = jnp.broadcast_to(inverse, edge_inv.shape)
-    edge_agg = (summed * inverse).astype(BF)
-
-    forward_params(patient)
-    for copy in par_urgent:
-        copy.wait_recv()
     k_first = first_early * par_rows
-    norm_row = (n_dom - 1) * par_rows + rows_all - 2 - shard * (n_dom - 1) // HID
     w_zero = []
     for c in range(2):
         rows_t = dot(place[:ROW_ONE, :k_first], par_rx[c, :k_first, :]).T
         w_zero.append(rows_t.astype(BF))
-        block = norm_row // 16 * 16
-        norms = par_rx[c, block : block + 32, :].astype(F32) if block + 32 <= k_all else (
-            par_rx[c, k_all - 32 : k_all, :].astype(F32)
-        )
-        block = min(block, k_all - 32)
-        norms_t = jnp.concatenate([norms, jnp.zeros((LANES - 32, HID), F32)], axis=0).T
+        norms_t = jnp.concatenate(
+            [norm_rx[c].astype(F32), jnp.zeros((LANES - 16, HID), F32)], axis=0
+        ).T
         for k in range(2):
-            lane = norm_row - block + k
+            lane = norm_local - norm_block + k
             col = norms_t[:, lane : lane + 1]
             norm_col[c * HALF_HID : (c + 1) * HALF_HID, 2 * k : 2 * k + 1] = col[:HALF_HID]
             norm_col[c * HALF_HID : (c + 1) * HALF_HID, 2 * k + 1 : 2 * k + 2] = col[HALF_HID:]
@@ -435,21 +474,20 @@
             wmat[c] = rows.astype(BF)
             wmat_t[c] = rows.T.astype(BF)
 
-    node = iota((HID, 48), 0)
-    first_row = lax.shift_right_logical(node * CLS, 8)
-    row_id = iota((HID, 48), 1)
-    pick_a = jnp.where(row_id == first_row, 1.0, 0.0)
-    pick_b = jnp.where(row_id == first_row + 1, 1.0, 0.0)
-    start_lane = (iota((HID, HID), 0) * CLS) & (HID - 1)
-    lane_w = iota((HID, HID), 1)
+    place_row = iota((2 * 48, HID), 0)
+    flat_row = jnp.where(place_row < 48, 2 * place_row, 2 * (place_row - 48) + 1)
+    first_row = lax.shift_right_logical(iota((2 * 48, HID), 1) * CLS, 7)
+    pick_a = jnp.where(flat_row == first_row, 1.0, 0.0).astype(BF)
+    pick_b = jnp.where(flat_row == first_row + 1, 1.0, 0.0).astype(BF)
+    start_lane = (iota((HID, LANES), 0) * CLS) & (LANES - 1)
+    lane_w = iota((HID, LANES), 1)
 
     def assemble_head():
         for c in range(2):
             flat = dot(place[ROW_TWO:ROW_NORM, :], par_rx[c]).astype(BF)
-            lo, hi = dot(pick_a.astype(BF), flat), dot(pick_b.astype(BF), flat)
-            wide = jnp.where(lane_w >= start_lane, lo, hi)
-            wide = roll_rows(wide, start_lane, False)
-            head = jnp.where(lane_w < CLS, wide, 0.0)[:, :LANES]
+            flat = jnp.concatenate([flat[:, :LANES], flat[:, LANES:]], axis=0)
+            wide = jnp.where(lane_w >= start_lane, dot(pick_a, flat, 0, 0), dot(pick_b, flat, 0, 0))
+            head = jnp.where(lane_w < CLS, roll_rows(wide, start_lane, False), 0.0)
             head_t = head.T[:CLS_PAD]
             half_rows = slice(c * HALF_HID, (c + 1) * HALF_HID)
             head_ws[half_rows, :] = head[:HALF_HID].astype(BF)
@@ -489,65 +527,87 @@
 
         loop(half // (2 * LANES), body)
 
-    def norm_edge(layer):
-        def body(j):
-            cols = pl.ds(pl.multiple_of(j * LANES, LANES), LANES)
-            edge_h[layer, :, cols] = norm_apply(edge_mixed[:, cols], layer)[2]
-
-        loop(halo // LANES, body)
+    def norm_edge(layer, mix):
+        for j in range(halo // LANES):
+            cols = slice(j * LANES, (j + 1) * LANES)
+            edge_h[layer, :, cols] = norm_apply(mix(cols), layer)[2]
+
         pack_halo(1 + layer, edge_h[layer].astype(F32).T)
         send_halo(1 + layer)
 
     def rows_of(x, agg):
         return jnp.concatenate([x[:FEAT_PAD], agg[:FEAT_PAD], x[FEAT_PAD:], agg[FEAT_PAD:]], axis=0)
 
-    x_own = xs[:, own_cols]
-    agg_own = agg_zero[...]
-    edge_mixed[...] = dot(w_zero, rows_of(edge_x[...], edge_agg))
-    norm_edge(0)
-    norm_forward(
-        0, lambda c: dot(
-            w_zero,
-            rows_of(
-                xs[:, pl.ds(pl.multiple_of(own + c, wide_cols), wide_cols)],
-                agg_zero[:, c : c + wide_cols],
-            ),
-        ),
-    )
-    h_pair_one = pair_copy(hs.at[0, :, own_cols], hs.at[0, :, own_cols], 2)
-    h_pair_one.start()
-    mixed[...] = dot(hs[0, :, own_cols], a_rows[:, own_cols], 1, 1)
+    def aggregate_zero(summed, inv_at, cols):
+        inverse = 1.0 / jnp.maximum(summed[fin : fin + 1, :], 1.0)
+        inv_at[:, cols] = jnp.broadcast_to(inverse, (8, summed.shape[1]))
+        return (summed * inverse).astype(BF)
+
+    def shifted_cols(cols):
+        return slice(half + cols.start, half + cols.stop)
+
+    def own_chunk(c):
+        return pl.ds(pl.multiple_of(own + c, wide_cols), wide_cols)
+
+    def mix_edge_zero(cols):
+        agg = aggregate_zero(
+            mixed[0:LANES, shifted_cols(cols)] + dot(halo_zero, edge_hm[:, cols]), edge_inv, cols
+        )
+        return dot(w_zero, rows_of(edge_x[:, cols], agg))
+
+    def mix_zero(c):
+        cols = slice(c, c + wide_cols)
+        agg = aggregate_zero(
+            mixed[0:LANES, cols] + dot(halo_zero, hmt[:, own_chunk(c)]), inv_ref, cols
+        )
+        agg_zero[:, cols] = agg
+        return dot(w_zero, rows_of(xs[:, own_chunk(c)], agg))
+
+    norm_edge(0, mix_edge_zero)
     wait_params(patient)
     par_rest = par_pairs(patient, 20)
     for copy in par_rest:
         copy.start()
+    norm_forward(0, mix_zero)
+    h_pair_one = pair_copy(hs.at[0, :, own_cols], hs.at[0, :, own_cols], 2)
+    h_pair_one.start()
+    mixed[:, : half + halo] = dot(hs[0, :, own_cols], a_rows[:, own_cols], 1, 1)
     for copy in par_rest:
         copy.wait_recv()
     assemble_hidden()
     w_self_t = jnp.concatenate([wmat_t[0, :, :LANES], wmat_t[1, :, :LANES]], axis=1)
     w_neigh_t = jnp.concatenate([wmat_t[0, :, LANES:], wmat_t[1, :, LANES:]], axis=1)
     h_pair_one.wait_recv()
-    mixed[...] += dot(hs[0, :, far_cols], a_rows[:, far_cols], 1, 1)
-    edge_mixed[...] = dot(hs[0], edge_rows[...], 1, 1)
+    mixed[:, : half + halo] += dot(hs[0, :, far_cols], a_rows[:, far_cols], 1, 1)
     wait_halo(1)
     halo_one = read_halo(1)
-    edge_agg = ((edge_mixed[...] + dot(halo_one, edge_hm[...])) * edge_inv[0:1, :]).astype(BF)
-    edge_mixed[...] = dot(w_self_t, edge_h[0]) + dot(w_neigh_t, edge_agg)
-    norm_edge(1)
-    agg_ref[0] = ((mixed[...] + dot(halo_one, hmt[:, own_cols])) * inv_ref[0:1, :]).astype(BF)
-    norm_forward(
-        1, lambda c: dot(w_self_t, hs[0, :, pl.ds(pl.multiple_of(own + c, wide_cols), wide_cols)])
-        + dot(w_neigh_t, agg_ref[0, :, c : c + wide_cols]),
-    )
+
+    def mix_edge_one(cols):
+        summed = mixed[:, shifted_cols(cols)] + dot(halo_one, edge_hm[:, cols])
+        agg = (summed * edge_inv[0:1, cols]).astype(BF)
+        return dot(w_self_t, edge_h[0, :, cols]) + dot(w_neigh_t, agg)
+
+    def mix_one(c):
+        return dot(w_self_t, hs[0, :, own_chunk(c)]) + dot(
+            w_neigh_t, agg_ref[0, :, c : c + wide_cols]
+        )
+
+    norm_edge(1, mix_edge_one)
+    total = mixed[:, :half] + dot(halo_one, hmt[:, own_cols])
+    agg_ref[0] = (total * inv_ref[0:1, :]).astype(BF)
+    norm_forward(1, mix_one)
     h_pair_two = pair_copy(hs.at[1, :, own_cols], hs.at[1, :, own_cols], 3)
     h_pair_two.start()
-    mixed[...] = dot(hs[1, :, own_cols], a_rows[:, own_cols], 1, 1)
+    mixed[:, :half] = dot(hs[1, :, own_cols], a_rows[:half, own_cols], 1, 1)
     assemble_head()
     h_pair_two.wait_recv()
-    mixed[...] += dot(hs[1, :, far_cols], a_rows[:, far_cols], 1, 1)
+    mixed[:, :half] += dot(hs[1, :, far_cols], a_rows[:half, far_cols], 1, 1)
     wait_halo(2)
-    total = mixed[...] + dot(read_halo(2), hmt[:, own_cols])
-    agg_ref[1] = (total * inv_ref[0:1, :]).astype(BF)
+    halo_two = read_halo(2)
+    for c in range(0, half, wide_cols):
+        cols = slice(c, c + wide_cols)
+        total = mixed[:, cols] + dot(halo_two, hmt[:, own_chunk(c)])
+        agg_ref[1, :, cols] = (total * inv_ref[0:1, cols]).astype(BF)
 
     logits = dot(head_ws_t[...], hs[1, :, own_cols]) + dot(head_wn_t[...], agg_ref[1])
     class_id = iota((CLS_PAD, half), 0)
@@ -571,26 +631,25 @@
         part_tx[...] = dot(hmt[:, own_cols], gs_all[k, :, own_cols], 1, 1)
         part = pair_copy(part_tx, part_rx.at[k], 8 + k)
         part.start()
-        whole.start()
         return whole, part
 
-    def send_back(k, part):
+    def send_back(k, part, whole):
         part.wait()
         pack_halo(3 + k, part_tx[...] + part_rx[k])
         send_halo(3 + k)
-
-    def spread(k, whole, between=None):
-        mixed[...] += dot(gs_all[k, :, own_cols], a_rows[:, own_cols])
-        if between is not None:
-            between()
-        whole.wait_recv()
-        mixed[...] += dot(gs_all[k, :, far_cols], b_far[...])
+        whole.start()
+
+    def spread(k, whole, base):
+        mixed[:, :half] = dot(gs_all[k, :, own_cols], a_rows[:half, own_cols])
         if k == 1:
             norm_slope(0)
+        whole.wait_recv()
+        mixed[:, half : 2 * half] = dot(gs_all[k, :, far_cols], b_far[...])
+        mixed[:, :half] = mixed[:, :half] + mixed[:, half : 2 * half] + base()
         wait_halo(3 + k)
         return read_halo(3 + k)
 
-    def norm_backward(layer, back):
+    def norm_backward(layer, back, after=None):
         acc_gain[...] = jnp.zeros_like(acc_gain)
         acc_bias[...] = jnp.zeros_like(acc_bias)
 
@@ -598,8 +657,8 @@
         for j in range(n_cols):
             cols = slice(j * wide_cols, (j + 1) * wide_cols)
             n = normed[layer, :, cols]
-            own_chunk = pl.ds(pl.multiple_of(own + j * wide_cols, wide_cols), wide_cols)
-            g_shift = (mixed[:, cols] + dot(back, sel[:, own_chunk])) * slope[layer, :, cols]
+            through = mixed[:, cols] + dot(back, sel[:, own_chunk(j * wide_cols)])
+            g_shift = through * slope[layer, :, cols]
             scaled = g_shift * n
             acc_gain[...] += scaled[:, :LANES] + scaled[:, LANES:]
             acc_bias[...] += g_shift[:, :LANES] + g_shift[:, LANES:]
@@ -607,7 +666,10 @@
             mean_one = jnp.mean(gn, axis=0, keepdims=True)
             mean_two = jnp.mean(gn * n, axis=0, keepdims=True)
             g_mixed = (gn - mean_one - n * mean_two) * scale_inv[layer, 0:1, cols]
-            g_low[:, cols] = g_mixed.astype(BF)
+            g_chunk = g_mixed.astype(BF)
+            g_low[:, cols] = g_chunk
+            if after is not None:
+                after(cols, own_chunk(j * wide_cols), g_chunk)
 
         gain_row = jnp.sum(acc_gain[...].T, axis=0, keepdims=True)
         bias_row = jnp.sum(acc_bias[...].T, axis=0, keepdims=True)
@@ -681,38 +743,35 @@
 
     gs_all[0, :, own_cols] = (dot(head_wn[:, :CLS_PAD], g_head) * inv_ref[0:1, :]).astype(BF)
     g_pair_two, part_two = exchange_backward(0)
-    mixed[...] = dot(head_ws[:, :CLS_PAD], g_head)
     dws = dot(hs[1, :, own_cols], g_head, 1, 1)
     dwn = dot(agg_ref[1], g_head, 1, 1)
     norm_slope(1)
-    send_back(0, part_two)
-    lane_h = iota((HID, HID), 1)
+    send_back(0, part_two, g_pair_two)
+    dw_head[...] = jnp.zeros_like(dw_head)
     for c in range(2):
         piece = slice(c * HALF_HID, (c + 1) * HALF_HID)
-        dw_head[...] = jnp.zeros_like(dw_head)
         dw_head[:HALF_HID, :CLS_PAD] = dws[piece]
         dw_head[HALF_HID:, :CLS_PAD] = dwn[piece]
         wide = roll_rows(dw_head[...], start_lane, True)
-        low_part = jnp.where(lane_h >= start_lane, wide, 0.0)
-        high_part = jnp.where(lane_h >= start_lane, 0.0, wide)
-        flat = dot(pick_a, low_part, 0, 0, lax.Precision.HIGHEST) + dot(
-            pick_b, high_part, 0, 0, lax.Precision.HIGHEST
-        )
+        low_part = jnp.where(lane_w >= start_lane, wide, 0.0)
+        high_part = jnp.where(lane_w >= start_lane, 0.0, wide)
+        stacked = jnp.concatenate([*parts(low_part), *parts(high_part)], axis=0)
+        picks = jnp.concatenate([pick_a] * 3 + [pick_b] * 3, axis=1)
+        flat = dot(picks, stacked)
+        flat = jnp.concatenate([flat[:48], flat[48:]], axis=1)
         base = 2 * fin + 2 * HALF_HID
         grads[c, base : base + HEAD_ROWS, :] = flat[:HEAD_ROWS]
-    back = spread(0, g_pair_two)
-    norm_backward(1, back)
-
+    back = spread(0, g_pair_two, lambda: dot(head_ws[:, :CLS_PAD], g_head))
+    w_self = jnp.concatenate([wmat[0, :LANES], wmat[1, :LANES]], axis=0)
+    w_neigh = jnp.concatenate([wmat[0, LANES:], wmat[1, LANES:]], axis=0)
+
+    def through_one(cols, own_part, g):
+        gs_all[1, :, own_part] = (dot(w_neigh, g) * inv_ref[0:1, cols]).astype(BF)
+
+    norm_backward(1, back, through_one)
+
+    g_pair_one, part_one = exchange_backward(1)
     g_one = g_low[...]
-    w_self = jnp.concatenate(
-        [wmat[0, :LANES], wmat[1, :LANES]], axis=0
-    )
-    w_neigh = jnp.concatenate(
-        [wmat[0, LANES:], wmat[1, LANES:]], axis=0
-    )
-    gs_all[1, :, own_cols] = (dot(w_neigh, g_one) * inv_ref[0:1, :]).astype(BF)
-    g_pair_one, part_one = exchange_backward(1)
-    mixed[...] = dot(w_self, g_one)
     dws = dot(hs[0, :, own_cols], g_one, 1, 1)
     dwn = dot(agg_ref[0], g_one, 1, 1)
     for c in range(2):
@@ -730,13 +789,14 @@
         early_rx.at[pl.ds(early_start, early_rows), :], 6,
     )
     early_pair.start()
-    send_back(1, part_one)
-    back = spread(1, g_pair_one, early_out)
+    send_back(1, part_one, g_pair_one)
+    early_out()
+    back = spread(1, g_pair_one, lambda: dot(w_self, g_low[...]))
     norm_backward(0, back)
 
     g_zero = g_low[...]
-    dws = dot(x_own, g_zero, 1, 1)
-    dwn = dot(agg_own, g_zero, 1, 1)
+    dws = dot(xs[:, own_cols], g_zero, 1, 1)
+    dwn = dot(agg_zero[...], g_zero, 1, 1)
     for c in range(2):
         start = c * FEAT_PAD
         grads[c, 0:fin, :] = dws[start : start + fin]
@@ -750,7 +810,6 @@
     ]
     for copy in late_pairs:
         copy.start()
-    stage_two(range(first_early, n_dom))
     for copy in late_pairs:
         copy.wait_recv()
     stage_one(range(first_early), late_rx)
@@ -765,6 +824,7 @@
     def _():
         top_copy(0, top_one.at[low], high * group + group - 1).start()
 
+    stage_two(range(first_early, n_dom))
     stage_two(range(first_early))
 
     @pl.when(low == group - 1)
@@ -803,7 +863,7 @@
 
     for copy in (
         x_pair, h_pair_one, h_pair_two, g_pair_two, g_pair_one,
-        *par_urgent, *par_rest, *late_pairs,
+        *par_rest, *late_pairs,
     ):
         copy.wait_send()
     for k in range(3, 5):
@@ -819,8 +879,21 @@
 
     part = pl.ds(0, n_dom - n_high)
     pltpu.make_async_copy(one_tx.at[part], one_tx.at[part], one_send).wait()
-    part = pl.ds(0, (n_dom - 1) * par_rows)
-    pltpu.make_async_copy(par_rx.at[f, part, :], par_rx.at[f, part, :], par_send).wait()
+    n_sent = n_high - 1 + len(urgent) * (2 * group - 1) + len(patient) * (group - 1)
+    while n_sent > 0:
+        part = pl.ds(0, min(n_sent, n_dom) * par_rows)
+        pltpu.make_async_copy(par_rx.at[f, part, :], par_rx.at[f, part, :], par_send).wait()
+        n_sent -= n_dom
+
+    @pl.when(me == n_dom - 1)
+    def _():
+        for step in range(1, n_high):
+            pltpu.make_async_copy(norm_own, norm_own, norm_send.at[0]).wait()
+
+    @pl.when(last_low)
+    def _():
+        for step in range(2 * group - 1):
+            pltpu.make_async_copy(norm_own, norm_own, norm_send.at[1]).wait()
 
 
 def round_up(value, step):
@@ -841,12 +914,12 @@
     head_end = 2 * fin + 2 * HALF_HID + HEAD_ROWS
     first_early = -(-2 * fin * HID // shard)
     assert shard * (n_dom - 1) <= (rows_all - 2) * HID and rows_all % 8 > 2
-    urgent = sorted({d // group for d in range(first_early)} | {n_dom // group - 1})
+    urgent = sorted({d // group for d in range(first_early)})
     cfg = dict(
         group=group, first_early=first_early, urgent=urgent,
         n_dom=n_dom, nodes=nodes, half=half, halo=halo, shard=shard, fin=fin, win=win,
         par_rows=par_rows, rows_all=rows_all, grad_rows=grad_rows,
-        h_rows=min(nodes, 2**18 // halo), slots=half // LANES if halo <= 256 else 2,
+        h_rows=nodes if halo <= 256 else LANES, slots=half // LANES if halo <= 256 else 2,
     )
     hbm = pl.BlockSpec(memory_space=pl.ANY)
     vmem = pl.BlockSpec(memory_space=pltpu.VMEM)
@@ -860,7 +933,7 @@
         pltpu.VMEM((cfg["slots"], LANES, half), i32),
         pltpu.VMEM((cfg["h_rows"], halo), i32),
         pltpu.VMEM((fin, nodes), BF),
-        pltpu.VMEM((half, nodes), BF),
+        pltpu.VMEM((half + halo, nodes), BF),
         pltpu.VMEM((half, half), BF),
         pltpu.VMEM((halo, nodes), BF),
         pltpu.VMEM((halo, nodes), BF),
@@ -870,15 +943,13 @@
         pltpu.VMEM((2, HID, half), BF),
         pltpu.VMEM((LANES, half), BF),
         pltpu.VMEM((halo, nodes), BF),
-        pltpu.VMEM((halo, nodes), BF),
         pltpu.VMEM((halo, halo), BF),
         pltpu.VMEM((LANES, halo), BF),
         pltpu.VMEM((2, HID, halo), BF),
-        pltpu.VMEM((HID, halo), F32),
         pltpu.VMEM((8, halo), F32),
         pltpu.VMEM((halo, HID), F32),
         pltpu.VMEM((2, halo, HID), F32),
-        pltpu.VMEM((HID, half), F32),
+        pltpu.VMEM((HID, half + max(halo, half)), F32),
         pltpu.VMEM((2, HID, half), F32),
         pltpu.VMEM((2, HID, half), F32),
         pltpu.VMEM((2, 8, half), F32),
@@ -888,6 +959,7 @@
         pltpu.VMEM((2 * win, LANES), F32),
         pltpu.VMEM((par_rows, HID), BF),
         pltpu.VMEM((2, n_dom * par_rows, HID), BF),
+        pltpu.VMEM((2, 16, HID), BF),
         pltpu.VMEM((2, HID, HID), BF),
         pltpu.VMEM((2, HID, HID), BF),
         pltpu.VMEM((HID, 8), F32),
@@ -906,7 +978,7 @@
         pltpu.VMEM((2, 8, HID), F32),
         pltpu.VMEM((group, 8, HID), F32),
         pltpu.VMEM((n_dom // group, 8, HID), F32),
-        pltpu.VMEM((HID, HID), F32),
+        pltpu.VMEM((HID, LANES), F32),
         pltpu.VMEM((HID, LANES), F32),
         pltpu.VMEM((HID, LANES), F32),
         pltpu.VMEM((ROW_NORM, n_dom * par_rows), BF),
@@ -918,6 +990,8 @@
         pltpu.SemaphoreType.DMA,
         pltpu.SemaphoreType.DMA((n_dom // group,)),
         pltpu.SemaphoreType.DMA((n_dom // group,)),
+        pltpu.SemaphoreType.DMA((2,)),
+        pltpu.SemaphoreType.DMA((2,)),
         pltpu.SemaphoreType.DMA,
         pltpu.SemaphoreType.DMA((n_dom // group,)),
         pltpu.SemaphoreType.DMA,
@@ -946,15 +1020,28 @@
         label_mask.reshape(1, nodes),
         master,
     )
-    own_grad = grad
-    new_first = DECAY_ONE * first + (1.0 - DECAY_ONE) * own_grad
-    new_second = DECAY_TWO * second + (1.0 - DECAY_TWO) * own_grad * own_grad
-    first_hat = new_first / (1.0 - DECAY_ONE**STEP)
-    second_hat = new_second / (1.0 - DECAY_TWO**STEP)
-    new_master = master - LEARN_RATE * (
-        first_hat / (jnp.sqrt(second_hat) + ADAM_EPS) + WEIGHT_DECAY * master
-    )
-    return (scalars[0, 0], scalars[1, 0], new_master, new_first, new_second)
+    def finish(grad_ref, scalar_ref, master_ref, first_ref, second_ref, *outs):
+        loss_out, count_out, master_out, first_out, second_out = outs
+        own_grad = grad_ref[...]
+        new_first = DECAY_ONE * first_ref[...] + (1.0 - DECAY_ONE) * own_grad
+        new_second = DECAY_TWO * second_ref[...] + (1.0 - DECAY_TWO) * own_grad * own_grad
+        first_hat = new_first / (1.0 - DECAY_ONE**STEP)
+        second_hat = new_second / (1.0 - DECAY_TWO**STEP)
+        old = master_ref[...]
+        master_out[...] = old - LEARN_RATE * (
+            first_hat / (jnp.sqrt(second_hat) + ADAM_EPS) + WEIGHT_DECAY * old
+        )
+        first_out[...] = new_first
+        second_out[...] = new_second
+        loss_out[...] = scalar_ref[0:1, 0:1]
+        count_out[...] = scalar_ref[1:2, 0:1]
+
+    one, own_shape = jax.ShapeDtypeStruct((1, 1), F32), jax.ShapeDtypeStruct((1, shard), F32)
+    loss, count, *updated = pl.pallas_call(
+        finish, out_shape=(one, one, own_shape, own_shape, own_shape),
+        in_specs=[vmem] * 5, out_specs=(vmem,) * 5,
+    )(grad, scalars, master, first, second)
+    return (loss[0, 0], count[0, 0], *updated)
 
 
 def solution(mesh):

time: 57 us -> 53.9 us (0.946)
  other arithmetic: 1.55 us -> 0 us
  local copies, waits for them, and re-layouts: 1.27 us -> 0 us
    pallas_call x1, Pallas kernels: 53.4 us -> 51.6 us  [per_device(): pl.pallas_call(functools.partial(kernel, cfg), out_shape=(jax.ShapeDtypeS...]
    sub x1 -> x0, other arithmetic: 1.55 us -> none  [per_device(): master - LEARN_RATE * (first_hat / (jnp.sqrt(second_hat) + ADAM_EPS) + WE...]
    pallas_call x0 -> x1, Pallas kernels: none -> 1.45 us  [per_device(): pl.pallas_call(finish, out_shape=(one, one, own_shape, own_shape, own_sha...]
    slice x1 -> x0, local copies, waits for them, and re-layouts: 1.25 us -> none  [per_device(): return (scalars[0, 0], scalars[1, 0], new_master, new_first, new_second)]
where the time goes in v3:
time: 53.9 us; the launch traced here: 53.7 us
  Pallas kernels  53 us (98%)
  between operations  0.64 us (1%)
    pallas_call x1, Pallas kernels, per_device(): pl.pallas_call(functools.partial(kernel, cfg), out_shape=(jax.ShapeDtypeS...  51.6 us
    pallas_call x1, Pallas kernels, per_device(): pl.pallas_call(finish, out_shape=(one, one, own_shape, own_shape, own_sha...  1.45 us

profile of v3, /device:TPU:0, one launch (start us, length us, event | category | flops | bytes accessed | tf_op | source)
XLA Modules:
  0.0 53.7 jit_solution(11840047583088679381)
XLA Ops:
  0.6 51.6 %shard_map.128 = (f32[1,6480]{1,0:T(1,128)}, f32[2,128]{1,0:T(2,128)}) custom-call(bf16[50,2048]{1,0:T(8,128)(2,1)} %bitcast.8, s32[2048,2048]{1,0:T(8,128)} %lm_in.1, s32[2048,128]{1,0:T(8,128)} %hm_in.1, s32[8,16]{1,0:T(8,128)} %bitcast.11, s32[1,2048]{1,0:T(1,128)} %bitcast.9, s32[1,2048]{1,0:T(1,128)} %bitcast.10, f32[1,6480]{1,0:T(1,128)} %master_ref.1), custom_call_target="tpu_custom_call" | custom-call | tf_op jit(solution)/shard_map/pallas_call | solution.py:1002
  52.2 1.4 %shard_map.129 = (f32[1,1]{1,0:T(1,128)}, f32[1,1]{1,0:T(1,128)}, f32[1,6480]{1,0:T(1,128)}, f32[1,6480]{1,0:T(1,128)}, f32[1,6480]{1,0:T(1,128)}) custom-call(f32[1,6480]{1,0:T(1,128)} %get-tuple-element.12.grad_ref, f32[2,128]{1,0:T(2,128)} %get-tuple-element.13.scalar_ref, f32[1,6480]{1,0:T(1,128)} %master_ref.1, f32[1,6480]{1,0:T(1,128)} %first_ref.1, ...), custom_call_target="tpu_custom_call" | custom-call | tf_op jit(solution)/shard_map/pallas_call | solution.py:1040

commit v4 on v3

--- a/solution.py
+++ b/solution.py
@@ -80,7 +80,7 @@
     cfg,
     x_in, lm_in, hm_in, send_hbm, label_hbm, lmask_hbm, master_hbm,
     grad_out, scalar_out,
-    send_in, label_in, lmask_in, master_in,
+    send_in, label_in, lmask_in, master_in, shares,
     a_stage, b_stage, h_stage, x_stage,
     a_rows, b_far, hmt, sel, xs, hs, gs_all, agg_ref, agg_zero,
     edge_far, edge_hm, edge_x, edge_h, edge_inv, part_tx, part_rx,
@@ -114,7 +114,7 @@
 
     chunk = 128
     n_chunk = half // chunk
-    x_copy = pltpu.make_async_copy(x_in, x_stage, local_sem.at[4])
+    x_copy = pltpu.make_async_copy(x_in, x_stage, local_sem.at[6])
     x_copy.start()
     small_copies = [
         pltpu.make_async_copy(src, dst, local_sem.at[k])
@@ -129,7 +129,7 @@
 
     def h_copy(i):
         return pltpu.make_async_copy(
-            hm_in.at[pl.ds(i * h_rows, h_rows), :], h_stage, local_sem.at[5]
+            hm_in.at[pl.ds(i * h_rows, h_rows), :], h_stage, local_sem.at[7]
         )
 
     h_copy(0).start()
@@ -139,13 +139,13 @@
     def a_copy(i):
         return pltpu.make_async_copy(
             lm_in.at[pl.ds(pl.multiple_of(own + i * chunk, chunk), chunk), :],
-            a_stage.at[lax.rem(i, slots)], local_sem.at[6 + lax.rem(i, slots)],
+            a_stage.at[lax.rem(i, slots)], local_sem.at[8 + lax.rem(i, slots)],
         )
 
     def b_copy(i):
         return pltpu.make_async_copy(
             lm_in.at[pl.ds(pl.multiple_of(far + i * chunk, chunk), chunk), own_cols],
-            b_stage.at[lax.rem(i, slots)], local_sem.at[6 + slots + lax.rem(i, slots)],
+            b_stage.at[lax.rem(i, slots)], local_sem.at[8 + slots + lax.rem(i, slots)],
         )
 
     loop(slots, lambda i: a_copy(i).start())
@@ -283,11 +283,12 @@
         return jnp.where(lane_t + off_lane < LANES, near, after)
 
     small_copies[0].wait()
-    flat_t[...] = jnp.zeros_like(flat_t)
+    shares[...] = jnp.zeros_like(shares)
+
     for k in range(-(-shard // LANES)):
         width = min(LANES, shard - k * LANES)
-        flat_t[k : k + 1, 0:width] = master_in[0:1, k * LANES : k * LANES + width]
-    window = to_window(flat_t[...])
+        shares[k : k + 1, 0:width] = master_in[0:1, k * LANES : k * LANES + width]
+    window = to_window(shares[...])
     if par_rows > win:
         window = jnp.concatenate([window, jnp.zeros((par_rows - win, HID), F32)], axis=0)
     par_tx[...] = window.astype(BF)
@@ -556,18 +557,16 @@
         return dot(w_zero, rows_of(edge_x[:, cols], agg))
 
     def mix_zero(c):
-        cols = slice(c, c + wide_cols)
-        agg = aggregate_zero(
-            mixed[0:LANES, cols] + dot(halo_zero, hmt[:, own_chunk(c)]), inv_ref, cols
-        )
-        agg_zero[:, cols] = agg
-        return dot(w_zero, rows_of(xs[:, own_chunk(c)], agg))
+        return dot(w_zero, rows_of(xs[:, own_chunk(c)], agg_zero[:, c : c + wide_cols]))
 
     norm_edge(0, mix_edge_zero)
     wait_params(patient)
     par_rest = par_pairs(patient, 20)
     for copy in par_rest:
         copy.start()
+    agg_zero[...] = aggregate_zero(
+        mixed[0:LANES, :half] + dot(halo_zero, hmt[:, own_cols]), inv_ref, slice(0, half)
+    )
     norm_forward(0, mix_zero)
     h_pair_one = pair_copy(hs.at[0, :, own_cols], hs.at[0, :, own_cols], 2)
     h_pair_one.start()
@@ -649,7 +648,7 @@
         wait_halo(3 + k)
         return read_halo(3 + k)
 
-    def norm_backward(layer, back, after=None):
+    def norm_backward(layer, back):
         acc_gain[...] = jnp.zeros_like(acc_gain)
         acc_bias[...] = jnp.zeros_like(acc_bias)
 
@@ -666,10 +665,7 @@
             mean_one = jnp.mean(gn, axis=0, keepdims=True)
             mean_two = jnp.mean(gn * n, axis=0, keepdims=True)
             g_mixed = (gn - mean_one - n * mean_two) * scale_inv[layer, 0:1, cols]
-            g_chunk = g_mixed.astype(BF)
-            g_low[:, cols] = g_chunk
-            if after is not None:
-                after(cols, own_chunk(j * wide_cols), g_chunk)
+            g_low[:, cols] = g_mixed.astype(BF)
 
         gain_row = jnp.sum(acc_gain[...].T, axis=0, keepdims=True)
         bias_row = jnp.sum(acc_bias[...].T, axis=0, keepdims=True)
@@ -684,6 +680,10 @@
 
     norm_first = rows_all - 2
     top_start = rows_all // 8 * 8
+
+    def lay(ref, rows):
+        ref[:win, :] = rows[:, :LANES]
+        ref[win:, :] = rows[:, LANES:]
 
     def stage_one(doms, far_ref):
         loss_row = grads[f, rows_all : rows_all + 1, :] + far_ref[rows_all : rows_all + 1, :]
@@ -699,11 +699,11 @@
 
             @pl.when(low == to_low)
             def _():
-                one_rx[to_high, low] = rows
+                lay(one_rx.at[to_high, low], rows)
 
             @pl.when(low != to_low)
             def _():
-                one_tx[d] = rows
+                lay(one_tx.at[d], rows)
                 pltpu.make_async_remote_copy(
                     src_ref=one_tx.at[d], dst_ref=one_rx.at[to_high, low],
                     send_sem=one_send, recv_sem=one_recv.at[to_high],
@@ -765,10 +765,8 @@
     w_self = jnp.concatenate([wmat[0, :LANES], wmat[1, :LANES]], axis=0)
     w_neigh = jnp.concatenate([wmat[0, LANES:], wmat[1, LANES:]], axis=0)
 
-    def through_one(cols, own_part, g):
-        gs_all[1, :, own_part] = (dot(w_neigh, g) * inv_ref[0:1, cols]).astype(BF)
-
-    norm_backward(1, back, through_one)
+    norm_backward(1, back)
+    gs_all[1, :, own_cols] = (dot(w_neigh, g_low[...]) * inv_ref[0:1, :]).astype(BF)
 
     g_pair_one, part_one = exchange_backward(1)
     g_one = g_low[...]
@@ -793,7 +791,6 @@
     early_out()
     back = spread(1, g_pair_one, lambda: dot(w_self, g_low[...]))
     norm_backward(0, back)
-
     g_zero = g_low[...]
     dws = dot(xs[:, own_cols], g_zero, 1, 1)
     dwn = dot(agg_zero[...], g_zero, 1, 1)
@@ -850,16 +847,17 @@
         pltpu.make_async_copy(top_two.at[part], top_two.at[part], top_recv.at[1]).wait()
         norms = jnp.sum(top_two[...], axis=0)
         first = norm_first - shard * (n_dom - 1) // HID
-        two_rx[0, first : first + 2, :] += norms[norm_first - top_start : norm_first - top_start + 2]
-
-    total = jnp.sum(two_rx[...], axis=0)
-    scalar_out[0:1, :] = total[win - 1 : win, :LANES]
+        norms = norms[norm_first - top_start : norm_first - top_start + 2]
+        two_rx[0, first : first + 2, :] += norms[:, :LANES]
+        two_rx[0, win + first : win + first + 2, :] += norms[:, LANES:]
+
+    flat_t[...] = jnp.sum(two_rx[...], axis=0)
+    scalar_out[0:1, :] = jnp.broadcast_to(flat_t[win - 1 : win, 0:1], (1, LANES))
     scalar_out[1:2, :] = jnp.broadcast_to(label_count, (1, LANES))
-    total = jnp.where(iota((win, HID), 0) == win - 1, 0.0, total)
-    flat_t[...] = from_window(total)
+    shares[...] = from_window(jnp.concatenate([flat_t[:win, :], flat_t[win:, :]], axis=1))
     for k in range(-(-shard // LANES)):
         width = min(LANES, shard - k * LANES)
-        grad_out[0:1, k * LANES : k * LANES + width] = flat_t[k : k + 1, 0:width]
+        grad_out[0:1, k * LANES : k * LANES + width] = shares[k : k + 1, 0:width]
 
     for copy in (
         x_pair, h_pair_one, h_pair_two, g_pair_two, g_pair_one,
@@ -905,7 +903,7 @@
     half, shard, fin = nodes // 2, master.shape[1], features.shape[1]
     rows_all = n_dom * shard // HID
     span = (shard + HID - 2) // HID + 1
-    win = round_up(span + 1, 8)
+    win = round_up(span + 1, 4)
     par_rows = round_up(span, 16)
     grad_rows = round_up(rows_all + win, 8)
     group = 1
@@ -924,11 +922,13 @@
     hbm = pl.BlockSpec(memory_space=pl.ANY)
     vmem = pl.BlockSpec(memory_space=pltpu.VMEM)
     i32 = jnp.int32
+    pad = LANES if halo <= 256 else 0
     scratch = [
         pltpu.VMEM((8, n_dom), i32),
         pltpu.VMEM((1, nodes), i32),
         pltpu.VMEM((1, nodes), i32),
         pltpu.VMEM((1, shard), F32),
+        pltpu.VMEM((2 * win, LANES), F32),
         pltpu.VMEM((cfg["slots"], LANES, nodes), i32),
         pltpu.VMEM((cfg["slots"], LANES, half), i32),
         pltpu.VMEM((cfg["h_rows"], halo), i32),
@@ -949,9 +949,9 @@
         pltpu.VMEM((8, halo), F32),
         pltpu.VMEM((halo, HID), F32),
         pltpu.VMEM((2, halo, HID), F32),
-        pltpu.VMEM((HID, half + max(halo, half)), F32),
-        pltpu.VMEM((2, HID, half), F32),
-        pltpu.VMEM((2, HID, half), F32),
+        pltpu.VMEM((HID, half + max(halo, half) + pad), F32),
+        pltpu.VMEM((2, HID, half + pad), F32),
+        pltpu.VMEM((2, HID, half + pad), F32),
         pltpu.VMEM((2, 8, half), F32),
         pltpu.VMEM((8, half), F32),
         pltpu.VMEM((2, n_dom, 16, LANES), BF),
@@ -971,10 +971,10 @@
         pltpu.VMEM((2, grad_rows, HID), F32),
         pltpu.VMEM((grad_rows, HID), F32),
         pltpu.VMEM((grad_rows, HID), F32),
-        pltpu.VMEM((n_dom, win, HID), F32),
-        pltpu.VMEM((n_dom // group, group, win, HID), F32),
-        pltpu.VMEM((n_dom // group, win, HID), F32),
-        pltpu.VMEM((n_dom // group, win, HID), F32),
+        pltpu.VMEM((n_dom, 2 * win, LANES), F32),
+        pltpu.VMEM((n_dom // group, group, 2 * win, LANES), F32),
+        pltpu.VMEM((n_dom // group, 2 * win, LANES), F32),
+        pltpu.VMEM((n_dom // group, 2 * win, LANES), F32),
         pltpu.VMEM((2, 8, HID), F32),
         pltpu.VMEM((group, 8, HID), F32),
         pltpu.VMEM((n_dom // group, 8, HID), F32),
@@ -982,7 +982,7 @@
         pltpu.VMEM((HID, LANES), F32),
         pltpu.VMEM((HID, LANES), F32),
         pltpu.VMEM((ROW_NORM, n_dom * par_rows), BF),
-        pltpu.SemaphoreType.DMA((6 + 2 * cfg["slots"],)),
+        pltpu.SemaphoreType.DMA((8 + 2 * cfg["slots"],)),
         pltpu.SemaphoreType.DMA((24,)),
         pltpu.SemaphoreType.DMA((24,)),
         pltpu.SemaphoreType.DMA((5,)),

time: 53.9 us -> 53 us (0.983)
  Pallas kernels: 53 us -> 52.2 us
    pallas_call x1, Pallas kernels: 51.6 us -> 50.8 us  [per_device(): pl.pallas_call(functools.partial(kernel, cfg), out_shape=(jax.ShapeDtypeS...]
where the time goes in v4:
time: 53 us; the launch traced here: 52.9 us
  Pallas kernels  52.2 us (98%)
  between operations  0.64 us (1%)
    pallas_call x1, Pallas kernels, per_device(): pl.pallas_call(functools.partial(kernel, cfg), out_shape=(jax.ShapeDtypeS...  50.8 us
    pallas_call x1, Pallas kernels, per_device(): pl.pallas_call(finish, out_shape=(one, one, own_shape, own_shape, own_sha...  1.45 us

profile of v4, /device:TPU:0, one launch (start us, length us, event | category | flops | bytes accessed | tf_op | source)
XLA Modules:
  0.0 52.9 jit_solution(5562088593508485562)
XLA Ops:
  0.6 50.8 %shard_map.128 = (f32[1,6480]{1,0:T(1,128)}, f32[2,128]{1,0:T(2,128)}) custom-call(bf16[50,2048]{1,0:T(8,128)(2,1)} %bitcast.8, s32[2048,2048]{1,0:T(8,128)} %lm_in.1, s32[2048,128]{1,0:T(8,128)} %hm_in.1, s32[8,16]{1,0:T(8,128)} %bitcast.11, s32[1,2048]{1,0:T(1,128)} %bitcast.9, s32[1,2048]{1,0:T(1,128)} %bitcast.10, f32[1,6480]{1,0:T(1,128)} %master_ref.1), custom_call_target="tpu_custom_call" | custom-call | tf_op jit(solution)/shard_map/pallas_call | solution.py:1002
  51.4 1.4 %shard_map.129 = (f32[1,1]{1,0:T(1,128)}, f32[1,1]{1,0:T(1,128)}, f32[1,6480]{1,0:T(1,128)}, f32[1,6480]{1,0:T(1,128)}, f32[1,6480]{1,0:T(1,128)}) custom-call(f32[1,6480]{1,0:T(1,128)} %get-tuple-element.12.grad_ref, f32[2,128]{1,0:T(2,128)} %get-tuple-element.13.scalar_ref, f32[1,6480]{1,0:T(1,128)} %master_ref.1, f32[1,6480]{1,0:T(1,128)} %first_ref.1, ...), custom_call_target="tpu_custom_call" | custom-call | tf_op jit(solution)/shard_map/pallas_call | solution.py:1040

commit v5 on v4

--- a/solution.py
+++ b/solution.py
@@ -518,15 +518,12 @@
             hs[layer, :, out] = value
 
     def norm_slope(layer):
-        def body(i):
-            for j in range(2):
-                cols = pl.ds(pl.multiple_of((2 * i + j) * LANES, LANES), LANES)
-                shifted = normed[layer, :, cols] * norm_col[
-                    :, 2 * layer : 2 * layer + 1
-                ] + norm_col[:, 2 * layer + 1 : 2 * layer + 2]
-                slope[layer, :, cols] = gelu_grad(shifted)
-
-        loop(half // (2 * LANES), body)
+        for c in range(0, half, wide_cols):
+            cols = slice(c, c + wide_cols)
+            shifted = normed[layer, :, cols] * norm_col[
+                :, 2 * layer : 2 * layer + 1
+            ] + norm_col[:, 2 * layer + 1 : 2 * layer + 2]
+            slope[layer, :, cols] = gelu_grad(shifted)
 
     def norm_edge(layer, mix):
         for j in range(halo // LANES):
@@ -640,8 +637,7 @@
 
     def spread(k, whole, base):
         mixed[:, :half] = dot(gs_all[k, :, own_cols], a_rows[:half, own_cols])
-        if k == 1:
-            norm_slope(0)
+        norm_slope(1 - k)
         whole.wait_recv()
         mixed[:, half : 2 * half] = dot(gs_all[k, :, far_cols], b_far[...])
         mixed[:, :half] = mixed[:, :half] + mixed[:, half : 2 * half] + base()
@@ -685,7 +681,11 @@
         ref[:win, :] = rows[:, :LANES]
         ref[win:, :] = rows[:, LANES:]
 
-    def stage_one(doms, far_ref):
+    whole_window = [slice(0, 2 * win)]
+    cut = 2 * win // 16 * 8
+    two_parts = [slice(0, cut), slice(cut, 2 * win)]
+
+    def stage_one(doms, far_ref, pieces):
         loss_row = grads[f, rows_all : rows_all + 1, :] + far_ref[rows_all : rows_all + 1, :]
         row = iota((win, HID), 0)
         for d in doms:
@@ -695,20 +695,25 @@
             if d == n_dom - 1:
                 rows = jnp.where(row >= norm_first - start, 0.0, rows)
             rows = jnp.where(row == win - 1, loss_row, rows)
-            to_high, to_low = d // group, d % group
-
-            @pl.when(low == to_low)
+
+            @pl.when(low == d % group)
             def _():
-                lay(one_rx.at[to_high, low], rows)
-
-            @pl.when(low != to_low)
+                lay(one_rx.at[d // group, low], rows)
+
+            @pl.when(low != d % group)
             def _():
                 lay(one_tx.at[d], rows)
-                pltpu.make_async_remote_copy(
-                    src_ref=one_tx.at[d], dst_ref=one_rx.at[to_high, low],
-                    send_sem=one_send, recv_sem=one_recv.at[to_high],
-                    device_id=(high * group + to_low, f), device_id_type=MESH,
-                ).start()
+
+        for n, piece in enumerate(pieces):
+            for d in doms:
+                to_high, to_low = d // group, d % group
+
+                @pl.when(low != to_low)
+                def _():
+                    send_to(
+                        high * group + to_low, f, one_tx.at[d, piece, :],
+                        one_rx.at[to_high, low, piece, :], one_send, one_recv.at[n, to_high],
+                    )
 
     def top_copy(k, dst, p):
         return pltpu.make_async_remote_copy(
@@ -716,36 +721,33 @@
             device_id=(p, f), device_id_type=MESH,
         )
 
-    def stage_two(doms):
-        for d in doms:
-            to_high, to_low = d // group, d % group
-
-            @pl.when(low == to_low)
-            def _():
-                part = pl.ds(0, group - 1)
-                pltpu.make_async_copy(
-                    one_rx.at[to_high, part], one_rx.at[to_high, part], one_recv.at[to_high]
-                ).wait()
-                total = jnp.sum(one_rx[to_high], axis=0)
-
-                @pl.when(high == to_high)
+    def stage_two(doms, pieces):
+        for n, piece in enumerate(pieces):
+            for d in doms:
+                to_high, to_low = d // group, d % group
+
+                @pl.when(low == to_low)
                 def _():
-                    two_rx[high] = total
-
-                @pl.when(high != to_high)
-                def _():
-                    two_tx[to_high] = total
-                    pltpu.make_async_remote_copy(
-                        src_ref=two_tx.at[to_high], dst_ref=two_rx.at[high],
-                        send_sem=two_send, recv_sem=two_recv, device_id=(d, f),
-                        device_id_type=MESH,
-                    ).start()
+                    got = one_rx.at[to_high, pl.ds(0, group - 1), piece, :]
+                    pltpu.make_async_copy(got, got, one_recv.at[n, to_high]).wait()
+                    total = jnp.sum(one_rx[to_high, :, piece, :], axis=0)
+
+                    @pl.when(high == to_high)
+                    def _():
+                        two_rx[high, piece, :] = total
+
+                    @pl.when(high != to_high)
+                    def _():
+                        two_tx[to_high, piece, :] = total
+                        send_to(
+                            d, f, two_tx.at[to_high, piece, :], two_rx.at[high, piece, :],
+                            two_send, two_recv,
+                        )
 
     gs_all[0, :, own_cols] = (dot(head_wn[:, :CLS_PAD], g_head) * inv_ref[0:1, :]).astype(BF)
     g_pair_two, part_two = exchange_backward(0)
     dws = dot(hs[1, :, own_cols], g_head, 1, 1)
     dwn = dot(agg_ref[1], g_head, 1, 1)
-    norm_slope(1)
     send_back(0, part_two, g_pair_two)
     dw_head[...] = jnp.zeros_like(dw_head)
     for c in range(2):
@@ -780,7 +782,7 @@
 
     def early_out():
         early_pair.wait()
-        stage_one(range(first_early, n_dom), early_rx)
+        stage_one(range(first_early, n_dom), early_rx, whole_window)
 
     early_pair = pair_copy(
         grads.at[other, pl.ds(early_start, early_rows), :],
@@ -809,7 +811,7 @@
         copy.start()
     for copy in late_pairs:
         copy.wait_recv()
-    stage_one(range(first_early), late_rx)
+    stage_one(range(first_early), late_rx, two_parts)
     norms = grads[f, top_rows, :] + late_rx[top_rows, :]
     top_tx[0] = norms
 
@@ -821,8 +823,8 @@
     def _():
         top_copy(0, top_one.at[low], high * group + group - 1).start()
 
-    stage_two(range(first_early, n_dom))
-    stage_two(range(first_early))
+    stage_two(range(first_early, n_dom), whole_window)
+    stage_two(range(first_early), two_parts)
 
     @pl.when(low == group - 1)
     def _():
@@ -993,7 +995,7 @@
         pltpu.SemaphoreType.DMA((2,)),
         pltpu.SemaphoreType.DMA((2,)),
         pltpu.SemaphoreType.DMA,
-        pltpu.SemaphoreType.DMA((n_dom // group,)),
+        pltpu.SemaphoreType.DMA((2, n_dom // group)),
         pltpu.SemaphoreType.DMA,
         pltpu.SemaphoreType.DMA,
         pltpu.SemaphoreType.DMA((2,)),

time: 53 us -> 52.7 us (level)
  no operation moved by 1% of the time
where the time goes in v5:
time: 52.7 us; the launch traced here: 52.5 us
  Pallas kernels  51.8 us (98%)
  between operations  0.64 us (1%)
    pallas_call x1, Pallas kernels, per_device(): pl.pallas_call(functools.partial(kernel, cfg), out_shape=(jax.ShapeDtypeS...  50.4 us
    pallas_call x1, Pallas kernels, per_device(): pl.pallas_call(finish, out_shape=(one, one, own_shape, own_shape, own_sha...  1.45 us

profile of v5, /device:TPU:0, one launch (start us, length us, event | category | flops | bytes accessed | tf_op | source)
XLA Modules:
  0.0 52.5 jit_solution(3895090762559525288)
XLA Ops:
  0.6 50.4 %shard_map.128 = (f32[1,6480]{1,0:T(1,128)}, f32[2,128]{1,0:T(2,128)}) custom-call(bf16[50,2048]{1,0:T(8,128)(2,1)} %bitcast.8, s32[2048,2048]{1,0:T(8,128)} %lm_in.1, s32[2048,128]{1,0:T(8,128)} %hm_in.1, s32[8,16]{1,0:T(8,128)} %bitcast.11, s32[1,2048]{1,0:T(1,128)} %bitcast.9, s32[1,2048]{1,0:T(1,128)} %bitcast.10, f32[1,6480]{1,0:T(1,128)} %master_ref.1), custom_call_target="tpu_custom_call" | custom-call | tf_op jit(solution)/shard_map/pallas_call | solution.py:1004
  51.0 1.4 %shard_map.129 = (f32[1,1]{1,0:T(1,128)}, f32[1,1]{1,0:T(1,128)}, f32[1,6480]{1,0:T(1,128)}, f32[1,6480]{1,0:T(1,128)}, f32[1,6480]{1,0:T(1,128)}) custom-call(f32[1,6480]{1,0:T(1,128)} %get-tuple-element.12.grad_ref, f32[2,128]{1,0:T(2,128)} %get-tuple-element.13.scalar_ref, f32[1,6480]{1,0:T(1,128)} %master_ref.1, f32[1,6480]{1,0:T(1,128)} %first_ref.1, ...), custom_call_target="tpu_custom_call" | custom-call | tf_op jit(solution)/shard_map/pallas_call | solution.py:1042

commit v6 on v5

--- a/solution.py
+++ b/solution.py
@@ -508,6 +508,12 @@
         ]
         return n, rs, gelu(shifted).astype(BF)
 
+    def h_part(layer, n):
+        cols = pl.ds(pl.multiple_of(own + n * (half // 2), half // 2), half // 2)
+        return pair_copy(hs.at[layer, :, cols], hs.at[layer, :, cols], 2 + layer + 12 * n)
+
+    h_pairs = [[h_part(layer, n) for n in range(2)] for layer in range(2)]
+
     def norm_forward(layer, mix):
         for j in range(n_cols):
             cols = slice(j * wide_cols, (j + 1) * wide_cols)
@@ -516,6 +522,8 @@
             scale_inv[layer, :, cols] = jnp.broadcast_to(rs, (8, wide_cols))
             out = pl.ds(pl.multiple_of(own + j * wide_cols, wide_cols), wide_cols)
             hs[layer, :, out] = value
+            if (j + 1) % (n_cols // 2) == 0:
+                h_pairs[layer][j // (n_cols // 2)].start()
 
     def norm_slope(layer):
         for c in range(0, half, wide_cols):
@@ -565,16 +573,15 @@
         mixed[0:LANES, :half] + dot(halo_zero, hmt[:, own_cols]), inv_ref, slice(0, half)
     )
     norm_forward(0, mix_zero)
-    h_pair_one = pair_copy(hs.at[0, :, own_cols], hs.at[0, :, own_cols], 2)
-    h_pair_one.start()
-    mixed[:, : half + halo] = dot(hs[0, :, own_cols], a_rows[:, own_cols], 1, 1)
+    mixed[:, :half] = dot(hs[0, :, own_cols], a_rows[:half, own_cols], 1, 1)
     for copy in par_rest:
         copy.wait_recv()
     assemble_hidden()
     w_self_t = jnp.concatenate([wmat_t[0, :, :LANES], wmat_t[1, :, :LANES]], axis=1)
     w_neigh_t = jnp.concatenate([wmat_t[0, :, LANES:], wmat_t[1, :, LANES:]], axis=1)
-    h_pair_one.wait_recv()
-    mixed[:, : half + halo] += dot(hs[0, :, far_cols], a_rows[:, far_cols], 1, 1)
+    for copy in h_pairs[0]:
+        copy.wait_recv()
+    mixed[:, half : half + halo] = dot(hs[0], a_rows[half:, :], 1, 1)
     wait_halo(1)
     halo_one = read_halo(1)
 
@@ -589,14 +596,14 @@
         )
 
     norm_edge(1, mix_edge_one)
+    mixed[:, :half] += dot(hs[0, :, far_cols], a_rows[:half, far_cols], 1, 1)
     total = mixed[:, :half] + dot(halo_one, hmt[:, own_cols])
     agg_ref[0] = (total * inv_ref[0:1, :]).astype(BF)
     norm_forward(1, mix_one)
-    h_pair_two = pair_copy(hs.at[1, :, own_cols], hs.at[1, :, own_cols], 3)
-    h_pair_two.start()
     mixed[:, :half] = dot(hs[1, :, own_cols], a_rows[:half, own_cols], 1, 1)
     assemble_head()
-    h_pair_two.wait_recv()
+    for copy in h_pairs[1]:
+        copy.wait_recv()
     mixed[:, :half] += dot(hs[1, :, far_cols], a_rows[:half, far_cols], 1, 1)
     wait_halo(2)
     halo_two = read_halo(2)
@@ -862,7 +869,7 @@
         grad_out[0:1, k * LANES : k * LANES + width] = shares[k : k + 1, 0:width]
 
     for copy in (
-        x_pair, h_pair_one, h_pair_two, g_pair_two, g_pair_one,
+        x_pair, *h_pairs[0], *h_pairs[1], g_pair_two, g_pair_one,
         *par_rest, *late_pairs,
     ):
         copy.wait_send()

time: 52.7 us -> 52.6 us (level)
  no operation moved by 1% of the time
where the time goes in v6:
time: 52.6 us; the launch traced here: 52.4 us
  Pallas kernels  51.8 us (98%)
  between operations  0.64 us (1%)
    pallas_call x1, Pallas kernels, per_device(): pl.pallas_call(functools.partial(kernel, cfg), out_shape=(jax.ShapeDtypeS...  50.3 us
    pallas_call x1, Pallas kernels, per_device(): pl.pallas_call(finish, out_shape=(one, one, own_shape, own_shape, own_sha...  1.45 us

profile of v6, /device:TPU:0, one launch (start us, length us, event | category | flops | bytes accessed | tf_op | source)
XLA Modules:
  0.0 52.4 jit_solution(10866446632116363300)
XLA Ops:
  0.6 50.3 %shard_map.128 = (f32[1,6480]{1,0:T(1,128)}, f32[2,128]{1,0:T(2,128)}) custom-call(bf16[50,2048]{1,0:T(8,128)(2,1)} %bitcast.8, s32[2048,2048]{1,0:T(8,128)} %lm_in.1, s32[2048,128]{1,0:T(8,128)} %hm_in.1, s32[8,16]{1,0:T(8,128)} %bitcast.11, s32[1,2048]{1,0:T(1,128)} %bitcast.9, s32[1,2048]{1,0:T(1,128)} %bitcast.10, f32[1,6480]{1,0:T(1,128)} %master_ref.1), custom_call_target="tpu_custom_call" | custom-call | tf_op jit(solution)/shard_map/pallas_call | solution.py:1011
  51.0 1.4 %shard_map.129 = (f32[1,1]{1,0:T(1,128)}, f32[1,1]{1,0:T(1,128)}, f32[1,6480]{1,0:T(1,128)}, f32[1,6480]{1,0:T(1,128)}, f32[1,6480]{1,0:T(1,128)}) custom-call(f32[1,6480]{1,0:T(1,128)} %get-tuple-element.12.grad_ref, f32[2,128]{1,0:T(2,128)} %get-tuple-element.13.scalar_ref, f32[1,6480]{1,0:T(1,128)} %master_ref.1, f32[1,6480]{1,0:T(1,128)} %first_ref.1, ...), custom_call_target="tpu_custom_call" | custom-call | tf_op jit(solution)/shard_map/pallas_call | solution.py:1049
